TPU v7x, 512 devices: a whole 4x4x16 slice. The times are simulated.
512 devices in a mesh: gx: 8 (over y, core), gy: 4 (over x), gz: 16 (over z).
Axes of the slice: x: 4, y: 4, z: 16, core: 2. Of those that a mesh axis runs over, the one named last changes fastest.
Arguments:
- sph_pos: float32 [3, 8, 16, 8, 2048], P(None, None, 'gx', 'gy', 'gz'), may hold values from 0 to 1
- sph_vel: float32 [3, 8, 16, 8, 2048], P(None, None, 'gx', 'gy', 'gz'), may hold values from -4 to 4
- sph_mass: float32 [8, 16, 8, 2048], P(None, 'gx', 'gy', 'gz'), may hold values from 0.5 to 2
- cell_count: int32 [16, 8, 2048], P('gx', 'gy', 'gz'), may hold values from 1 to 8
- grain_pos: float32 [3, 2, 16, 8, 2048], P(None, None, 'gx', 'gy', 'gz'), may hold values from 0 to 1
- grain_vel: float32 [3, 2, 16, 8, 2048], P(None, None, 'gx', 'gy', 'gz'), may hold values from -3 to 3
- grain_radius: float32 [2, 16, 8, 2048], P(None, 'gx', 'gy', 'gz'), may hold values from 0.3 to 0.6
- contact_pairs: int32 [2, 8, 4, 98304], P(None, 'gx', 'gy', 'gz'), may hold values from 0 to 4159, as said below
- contact_count: int32 [8, 4, 16], P('gx', 'gy', 'gz'), may hold values from 3072 to 6144, as said below
- iface_grain: int32 [8, 4, 256, 128], P('gx', 'gy', 'gz'), may hold values from 0 to 1023
- iface_offset: float32 [3, 8, 4, 256, 128], P(None, 'gx', 'gy', 'gz'), may hold values from -0.25 to 1.25
- pair_count: int32 [8, 4, 256], P('gx', 'gy', 'gz'), may hold values from 0 to 128, as said below
- iface_cell: int32 [8, 4, 256, 128], P('gx', 'gy', 'gz'), may hold values from 0 to 511
Outputs:
- sph_accel: float32 [3, 8, 16, 8, 2048], P(None, None, 'gx', 'gy', 'gz')
- grain_force: float32 [3, 2, 16, 8, 2048], P(None, None, 'gx', 'gy', 'gz')
- grain_stress: float32 [6, 2, 16, 8, 2048], P(None, None, 'gx', 'gy', 'gz')
Inputs may be any that keep to these rules, and one draw needn't show every extreme that they name: `contact_pairs`: row 0 names any grain of the brick; row 1 names a grain of the same or an adjacent grain cell in the extended brick, never grain i itself. `contact_count`: some brick is full in every draw. `pair_count`: in every brick column one water brick layer receives 128 live pairs from every grain brick layer.
All inputs are finite; a program needn't handle non-finite values.
Results may differ from a plain program's by a relative error of at most 0.0003.
Values sent between devices are 32-bit elements; how exact they have to be, the bound alone decides.
No kernel may reach another device: no remote copies, remote signals or barrier semaphores. Data moves between devices by JAX's collectives and lax.ppermute only.
A program may use at most 128 MiB of HBM per device.

v0:
```python
import math

import jax
import jax.numpy as jnp
from jax import lax
from jax.experimental import pallas as pl
from jax.experimental.pallas import tpu as pltpu
from jax.sharding import PartitionSpec as P

NORMING = 21.0 / (2.0 * math.pi)
REST_DENSITY = 6.0
GRAVITY = 1.0
DRAG_RATE = 2.0
SPRING = 20.0
SOFT_WIDTH = 0.2
DAMPING = 0.5
SOFTENING = 0.01
GRAIN_WEIGHT = 2.0
VOLUME_FACTOR = 4.0 * math.pi / 3.0
TINY = 1e-30

F32 = jnp.float32
BF16 = jnp.bfloat16
VM = pltpu.VMEM
SM = pltpu.SMEM

Y_GRAIN = 28
Y_RIM = 35
Y_TILES = 37
X_VEL = 24
X_GRAIN = 36
X_RIM = 43
X_TILES = 49
GRAIN_LANE = 56


def call(kernel, outs, scratch=(), ins=(), cost=None, alias=None, grid=None, out_specs=None):
    single = not isinstance(outs, (list, tuple))
    count = 1 if single else len(outs)
    if out_specs is None:
        out_specs = [pl.BlockSpec(memory_space=VM)] * count
    extra = {}
    if grid is not None:
        extra["grid"] = grid
    return pl.pallas_call(
        kernel,
        out_shape=outs,
        in_specs=list(ins),
        out_specs=out_specs[0] if single else out_specs,
        scratch_shapes=list(scratch),
        input_output_aliases=alias or {},
        compiler_params=pltpu.CompilerParams(vmem_limit_bytes=24 * 1024 * 1024),
        cost_estimate=cost,
        **extra,
    )


def cost(micros):
    return pl.CostEstimate(flops=int(micros * 4e6), bytes_accessed=int(micros * 2e6), transcendentals=0)


V = pl.BlockSpec(memory_space=VM)
S = pl.BlockSpec(memory_space=SM)


def shape(*dims):
    return jax.ShapeDtypeStruct(dims, F32)


def lanes():
    return lax.broadcasted_iota(jnp.int32, (8, 128), 1)


def subs():
    return lax.broadcasted_iota(jnp.int32, (8, 128), 0)


def roll(value, amount):
    amount = amount % 128
    return value if amount == 0 else pltpu.roll(value, amount, 1)


def spread(row):
    return jnp.broadcast_to(row, (8, 128))


def lane_gather(table, index):
    numbers = lax.GatherDimensionNumbers(
        offset_dims=(),
        collapsed_slice_dims=(1,),
        start_index_map=(1,),
        operand_batching_dims=(0,),
        start_indices_batching_dims=(0,),
    )
    return lax.gather(
        table,
        index[..., None],
        numbers,
        slice_sizes=(1, 1),
        mode=lax.GatherScatterMode.PROMISE_IN_BOUNDS,
    )


def rim_lane(field, layer, col):
    return (field * 2 + layer) * 4 + col


def split_rows(value):
    high = value.astype(BF16).astype(F32)
    return jnp.concatenate([high, value - high], axis=0)


def scatter_dot(left, hot):
    return lax.dot_general(
        left, hot, (((1,), (1,)), ((), ())), preferred_element_type=F32
    )


def hot_rows(row):
    ids = lax.broadcasted_iota(jnp.int32, (128, 128), 0)
    return jnp.where(ids == jnp.broadcast_to(row, (128, 128)), 1.0, 0.0).astype(BF16)


def pack_kernel(place, counts, pos, vel, mass, count, gpos, gvel, grad, grain, offset, send, own):
    lane = lanes()
    sub = subs()
    low = jnp.zeros((8, 128), F32)
    high = jnp.zeros((8, 128), F32)
    for col in range(4):
        for field in range(7):
            if field < 3:
                value = pos[pl.ds(field * 32 + col, 8, stride=4), :]
            elif field == 3:
                value = mass[pl.ds(col, 8, stride=4), :]
                value = jnp.where(sub < spread(count[pl.ds(col, 1), :]), value, 0.0)
            else:
                value = vel[pl.ds((field - 4) * 32 + col, 8, stride=4), :]
            own[col * 7 + field] = value
            for layer in range(2):
                at = rim_lane(field, layer, col)
                low = jnp.where(lane == at, roll(value, at - layer), low)
                high = jnp.where(lane == at, roll(value, at - 126 - layer), high)
    for field in range(7):
        if field < 3:
            value = gpos[pl.ds(field * 8, 8), :]
        elif field < 6:
            value = gvel[pl.ds((field - 3) * 8, 8), :]
        else:
            value = grad[...]
        own[Y_GRAIN + field] = value
        at = GRAIN_LANE + field
        low = jnp.where(lane == at, roll(value, at), low)
        high = jnp.where(lane == at, roll(value, at - 127), high)
    radius = grad[...]
    volume = VOLUME_FACTOR * radius * radius * radius
    tables = [gvel[pl.ds(field * 8, 8), :] for field in range(3)] + [volume]
    for group in range(2):
        index = grain[pl.ds(group * 8, 8), :]
        row = index >> 7
        at = index & 127
        found = [jnp.zeros((8, 128), F32) for _ in range(4)]
        for place_row in range(8):
            here = row == place_row
            for field in range(4):
                got = lane_gather(spread(tables[field][place_row : place_row + 1]), at)
                found[field] = jnp.where(here, got, found[field])
        alive = jnp.zeros((8, 128), jnp.int32)
        for peer in range(8):
            alive = jnp.where(sub == peer, counts[group * 8 + peer], alive)
        found[3] = jnp.where(lane < alive, found[3], 0.0)
        for field in range(3):
            send[pl.ds(group * 128 + field, 8, stride=16), :] = offset[
                pl.ds(field * 16 + group * 8, 8), :
            ]
        for field in range(4):
            send[pl.ds(group * 128 + 3 + field, 8, stride=16), :] = found[field]
        send[pl.ds(group * 128 + 7, 8, stride=16), :] = jnp.zeros((8, 128), F32)
    for peer in range(16):
        send[pl.ds(peer * 16 + 8, 8), :] = jnp.where(peer < place[2], low, high)


def rim_kernel(place, arrived, own_in, own):
    step = pl.program_id(0)
    layer = place[2]
    other = jnp.where(step == 0, layer - 1, layer + 1)
    inside = jnp.logical_and(other >= 0, other <= 15)
    start = pl.multiple_of(jnp.clip(other, 0, 15) * 16 + 8, 8)
    own[0] = jnp.where(inside, arrived[pl.ds(start, 8), :], 0.0)


def widen_kernel(own, ahead, behind, up, down):
    for send, a in ((up, 1), (down, 0)):
        for y in range(6):
            source = (ahead, own, behind)[y // 2]
            col = a * 2 + y % 2
            for field in range(4):
                send[y * 4 + field] = source[col * 7 + field]
        for y in range(4):
            source = (ahead, own, own, behind)[y]
            col = a * 2 + (1, 0, 1, 0)[y]
            for field in range(3):
                send[X_VEL + y * 3 + field] = source[col * 7 + 4 + field]
            for field in range(7):
                for slot in range(2):
                    send[X_GRAIN + field, pl.ds(slot * 4 + y, 1), :] = source[
                        Y_GRAIN + field, pl.ds(slot * 4 + col, 1), :
                    ]
        for part, source in enumerate((own, ahead, behind)):
            for side in range(2):
                send[X_RIM + part * 2 + side] = source[Y_RIM + side]


class Near:
    def __init__(self, own, ahead, behind, left, right):
        self.own, self.ahead, self.behind = own, ahead, behind
        self.left, self.right = left, right

    def part(self, y):
        return (1, 0, 2)[y // 2] if y // 2 != 1 else 0

    def main(self, field, x, y):
        if x in (1, 2):
            source = (self.ahead, self.own, self.behind)[y // 2]
            return source[((x - 1) * 2 + y % 2) * 7 + field]
        source = self.left if x == 0 else self.right
        if field < 4:
            return source[y * 4 + field]
        return source[X_VEL + (y - 1) * 3 + field - 4]

    def rim(self, side, x, y):
        part = (1, 0, 2)[y // 2]
        if x in (1, 2):
            return (self.own, self.ahead, self.behind)[part][Y_RIM + side]
        source = self.left if x == 0 else self.right
        return source[X_RIM + part * 2 + side]

    def rim_col(self, x, y):
        return (1, 0, 1, 0)[x] * 2 + y % 2


def density_kernel(place, own, ahead, behind, left, right, out, near, table):
    lane = lanes()
    first = lane == 0
    last = lane == 127
    data = Near(own, ahead, behind, left, right)
    has_left = place[0] > 0
    has_right = place[0] < 7
    sign = jnp.where(lane < 64, -1.0, 1.0)
    packed = [[jnp.zeros((8, 128), F32) for _ in range(4)] for _ in range(3)]
    for x in range(4):
        for y in range(6):
            col = data.rim_col(x, y)
            rims = [data.rim(side, x, y) for side in range(2)]
            for field in range(4):
                value = data.main(field, x, y)
                edge = [rims[0], rims[1]]
                if field == 3 and x in (0, 3):
                    there = has_left if x == 0 else has_right
                    value = jnp.where(there, value, 0.0)
                    edge = [jnp.where(there, one, 0.0) for one in edge]
                shift = float(x - 1) if field == 0 else float(y - 2) if field == 1 else 0.0
                if shift:
                    value = value + shift
                    edge = [one + shift for one in edge]
                back = jnp.where(first, roll(edge[0], -rim_lane(field, 1, col)), roll(value, 1))
                fore = jnp.where(last, roll(edge[1], 127 - rim_lane(field, 0, col)), roll(value, 127))
                if field == 2:
                    back = back - 1.0
                    fore = fore + 1.0
                at = (x * 6 + y) * 12 + field
                near[at] = back
                near[at + 4] = value
                near[at + 8] = fore
                for side in range(2):
                    spot = side * 64 + x * 8 + y
                    here = lane == spot
                    outer = rim_lane(field, 0 if side == 0 else 1, col)
                    inner = rim_lane(field, 1 if side == 0 else 0, col)
                    packed[0][field] = jnp.where(here, roll(edge[side], spot - outer), packed[0][field])
                    packed[1][field] = jnp.where(here, roll(edge[side], spot - inner), packed[1][field])
                    packed[2][field] = jnp.where(
                        here, roll(value, spot - (0 if side == 0 else 127)), packed[2][field]
                    )
    packed[0][2] = packed[0][2] + sign
    packed[2][2] = packed[2][2] - sign
    for step_x in range(3):
        for step_y in range(3):
            for level in range(3):
                for field in range(4):
                    at = (24 + step_x * 3 + step_y) * 12 + level * 4 + field
                    near[at] = roll(packed[level][field], -((step_x - 1) * 8 + step_y - 1))
    for x in range(2):
        for y in range(4):
            for step in range(9):
                table[(x * 4 + y) * 9 + step] = (x + step // 3) * 6 + y + step % 3
    for step in range(9):
        table[72 + step] = 24 + step

    def one_column(target, carry):
        middle = table[target * 9 + 4] * 12
        center = [near[middle + 4 + field] for field in range(4)]

        def one_neighbour(step, total):
            base = table[target * 9 + step] * 12
            for level in range(3):
                for slot in range(8):
                    row = [
                        spread(near[base + level * 4 + field, pl.ds(slot, 1), :])
                        for field in range(4)
                    ]
                    dx = center[0] - row[0]
                    dy = center[1] - row[1]
                    dz = center[2] - row[2]
                    square = jnp.maximum(dx * dx + dy * dy + dz * dz, TINY)
                    radius = square * lax.rsqrt(square)
                    reach = jnp.maximum(1.0 - radius, 0.0)
                    reach = reach * reach
                    total = total + (reach * reach) * (4.0 * radius + 1.0) * row[3]
            return total

        total = lax.fori_loop(0, 9, one_neighbour, jnp.zeros((8, 128), F32))
        density = NORMING * total
        alive = center[3] > 0.0
        live = jnp.where(alive, 1.0, 0.0)
        safe = jnp.where(alive, density, 1.0)
        pressure = (density - REST_DENSITY) * live
        out[target * 3] = pressure / (safe * safe)
        out[target * 3 + 1] = live / safe
        out[target * 3 + 2] = pressure
        return carry

    lax.fori_loop(0, 9, one_column, 0)


def force_kernel(place, own, ahead, behind, left, right, fields, fleft, fright, reaction, out, near):
    lane = lanes()
    first = lane == 0
    last = lane == 127
    data = Near(own, ahead, behind, left, right)
    has_left = place[0] > 0
    has_right = place[0] < 7
    for x in range(4):
        for y in range(1, 5):
            col = data.rim_col(x, y)
            rims = [data.rim(side, x, y) for side in range(2)]
            source = fields if x in (1, 2) else fleft if x == 0 else fright
            far_x = (1, 0, 1, 0)[x]
            target = far_x * 4 + y - 1
            extra = []
            for which in range(2):
                value = source[target * 3 + which]
                halo = source[24 + which]
                extra.append((value, halo))
            levels = [[], [], []]
            for field in range(7):
                value = data.main(field, x, y)
                edge = [rims[0], rims[1]]
                if field == 3 and x in (0, 3):
                    there = has_left if x == 0 else has_right
                    value = jnp.where(there, value, 0.0)
                    edge = [jnp.where(there, one, 0.0) for one in edge]
                back = jnp.where(first, roll(edge[0], -rim_lane(field, 1, col)), roll(value, 1))
                fore = jnp.where(last, roll(edge[1], 127 - rim_lane(field, 0, col)), roll(value, 127))
                shift = float(x - 1) if field == 0 else float(y - 2) if field == 1 else 0.0
                if shift:
                    value, back, fore = value + shift, back + shift, fore + shift
                if field == 2:
                    back = back - 1.0
                    fore = fore + 1.0
                for level, one in enumerate((back, value, fore)):
                    levels[level].append(one)
            spot = (far_x + 1) * 8 + y
            for value, halo in extra:
                back = jnp.where(first, roll(halo, -spot), roll(value, 1))
                fore = jnp.where(last, roll(halo, 127 - 64 - spot), roll(value, 127))
                for level, one in enumerate((back, value, fore)):
                    levels[level].append(one)
            for level in range(3):
                px, py, pz, m, vx, vy, vz, press, inverse = levels[level]
                at = ((x * 4 + y - 1) * 3 + level) * 9
                for k, one in enumerate((px, py, pz, m, m * press, m * inverse, vx, vy, vz)):
                    near[at + k] = one

    def one_column(target, carry):
        a = target // 2
        b = target % 2
        middle = (((a + 1) * 4 + b + 1) * 3 + 1) * 9
        center = [near[middle + k] for k in range(3)]
        press = fields[(a * 4 + b + 1) * 3]
        inverse = fields[(a * 4 + b + 1) * 3 + 1]

        def one_neighbour(step, total):
            base = (((a + step // 3) * 4 + b + step % 3) * 3) * 9
            total = list(total)
            for level in range(3):
                for slot in range(8):
                    row = [
                        spread(near[base + level * 9 + k, pl.ds(slot, 1), :]) for k in range(9)
                    ]
                    dx = center[0] - row[0]
                    dy = center[1] - row[1]
                    dz = center[2] - row[2]
                    square = dx * dx + dy * dy + dz * dz
                    guarded = jnp.maximum(square, TINY)
                    radius = guarded * lax.rsqrt(guarded)
                    reach = jnp.maximum(1.0 - radius, 0.0)
                    cubed = reach * reach * reach
                    push = cubed * (row[3] * press + row[4])
                    soft = lax.rsqrt(square + SOFTENING)
                    drag = (cubed * row[5]) * (square * soft * soft)
                    total[0] = total[0] + push * dx
                    total[1] = total[1] + push * dy
                    total[2] = total[2] + push * dz
                    total[3] = total[3] + drag
                    total[4] = total[4] + drag * row[6]
                    total[5] = total[5] + drag * row[7]
                    total[6] = total[6] + drag * row[8]
            return tuple(total)

        zero = jnp.zeros((8, 128), F32)
        total = lax.fori_loop(0, 9, one_neighbour, (zero,) * 7)
        live = jnp.where(near[middle + 3] > 0.0, 1.0, 0.0)
        for d in range(3):
            slow = inverse * (near[middle + 6 + d] * total[3] - total[4 + d])
            force = 20.0 * NORMING * (total[d] - slow)
            if d == 2:
                force = force - GRAVITY
            out[pl.ds(d * 32 + target, 8, stride=4), :] = live * force + reaction[d * 4 + target]
        return carry

    lax.fori_loop(0, 4, one_column, 0)


def pair_kernel(own, fields, arrived, cells, send, reaction, left, hot):
    for peer in range(16):
        index = cells[pl.ds(peer, 1), :]
        at_row = index & 127
        at = spread(at_row)
        col_of = spread(index >> 7)
        found = None
        for col in range(4):
            mid = ((col // 2) * 4 + col % 2 + 1) * 3
            inverse = fields[mid + 1]
            tables = [own[col * 7 + k] for k in (0, 1, 2, 4, 5, 6)]
            tables += [own[col * 7 + 3] * inverse, fields[mid + 2], inverse]
            got = [lane_gather(one, at) for one in tables]
            if found is None:
                found = got
            else:
                here = col_of == col
                found = [jnp.where(here, new, old) for new, old in zip(got, found)]
        row = [spread(arrived[pl.ds(peer * 16 + k, 1), :]) for k in range(7)]
        delta = [row[d] - found[d] for d in range(3)]
        square = jnp.maximum(delta[0] * delta[0] + delta[1] * delta[1] + delta[2] * delta[2], TINY)
        radius = square * lax.rsqrt(square)
        reach = jnp.maximum(1.0 - radius, 0.0)
        cubed = reach * reach * reach
        weight = (DRAG_RATE * NORMING) * cubed * reach * (4.0 * radius + 1.0)
        push = (20.0 * NORMING) * found[7] * cubed
        hot[:, peer * 128 : peer * 128 + 128] = hot_rows(at_row)
        for d in range(3):
            bracket = row[6] * (push * delta[d] + weight * (found[3 + d] - row[3 + d]))
            send[peer, pl.ds(d, 1), :] = jnp.sum(found[6] * bracket, axis=0, keepdims=True)
            both = split_rows(-found[8] * bracket)
            col_both = jnp.concatenate([col_of, col_of], axis=0)
            for col in range(4):
                at16 = (d * 4 + col) * 16
                left[at16 : at16 + 16, peer * 128 : peer * 128 + 128] = jnp.where(
                    col_both == col, both, 0.0
                ).astype(BF16)
        send[peer, pl.ds(3, 1), :] = jnp.zeros((1, 128), F32)
    sums = scatter_dot(left[...], hot[...])
    for k in range(12):
        reaction[k] = sums[k * 16 : k * 16 + 8] + sums[k * 16 + 8 : k * 16 + 16]


def contact_kernel(place, live_count, own, ahead, behind, left, right, first, second, out, table, rims, turned, rows, lhs, hot):
    lane = lanes()
    sub = subs()
    has_left = place[0] > 0
    has_right = place[0] < 7
    for field in range(7):
        for slot in range(2):
            for x in range(4):
                for y in range(4):
                    if x in (1, 2):
                        source = (ahead, own, own, behind)[y]
                        value = source[
                            Y_GRAIN + field,
                            pl.ds(slot * 4 + (x - 1) * 2 + (1, 0, 1, 0)[y], 1),
                            :,
                        ]
                    else:
                        source, there = (left, has_left) if x == 0 else (right, has_right)
                        value = source[X_GRAIN + field, pl.ds(slot * 4 + y, 1), :]
                        value = jnp.where(there, value, 0.0)
                    table[pl.ds(field * 32 + slot * 16 + x * 4 + y, 1), :] = value
    for side in range(2):
        rims[...] = jnp.zeros((128, 128), F32)
        for part, source in enumerate((own, ahead, behind)):
            rims[pl.ds(part * 8, 8), :] = source[Y_RIM + side]
            rims[pl.ds((3 + part) * 8, 8), :] = jnp.where(
                has_left, left[X_RIM + part * 2 + side], 0.0
            )
            rims[pl.ds((6 + part) * 8, 8), :] = jnp.where(
                has_right, right[X_RIM + part * 2 + side], 0.0
            )
        turned[side] = jnp.transpose(rims[...])

    def one_group(group, carry):
        start = pl.multiple_of(group * 8, 8)
        one = first[pl.ds(start, 8), :]
        two = second[pl.ds(start, 8), :]
        own_row = one >> 7
        own_c = one & 127
        far_row = (two * 4033) >> 19
        far_c = two - far_row * 130
        far_slot = far_row >> 4
        far_x = (far_row >> 2) & 3
        far_y = far_row & 3
        far_at = jnp.clip(far_c - 1, 0, 127)
        x_part = jnp.where(far_x == 0, 1, jnp.where(far_x == 3, 2, 0))
        y_part = jnp.where(far_y == 0, 1, jnp.where(far_y == 3, 2, 0))
        rim_a = jnp.where(far_x == 0, 1, jnp.where(far_x == 3, 0, far_x - 1))
        rim_b = jnp.where(far_y == 0, 1, jnp.where(far_y == 3, 0, far_y - 1))
        rim_at = (x_part * 3 + y_part) * 8 + far_slot * 4 + rim_a * 2 + rim_b
        own_found = [jnp.zeros((8, 128), F32) for _ in range(7)]
        for row in range(8):
            here = own_row == row
            for field in range(7):
                got = lane_gather(spread(own[Y_GRAIN + field, pl.ds(row, 1), :]), own_c)
                own_found[field] = jnp.where(here, got, own_found[field])
        far_found = [jnp.zeros((8, 128), F32) for _ in range(7)]
        for row in range(32):
            here = far_row == row
            for field in range(7):
                got = lane_gather(spread(table[pl.ds(field * 32 + row, 1), :]), far_at)
                far_found[field] = jnp.where(here, got, far_found[field])
        for side, edge in ((0, 0), (1, 129)):
            here = far_c == edge
            for field in range(7):
                got = lane_gather(
                    spread(turned[side, pl.ds(GRAIN_LANE + field, 1), :]), rim_at
                )
                far_found[field] = jnp.where(here, got, far_found[field])
        shift = [
            (((own_row >> 1) & 1) - far_x + 1).astype(F32),
            ((own_row & 1) - far_y + 1).astype(F32),
            (own_c - far_c + 1).astype(F32),
        ]
        delta = [own_found[d] - far_found[d] + shift[d] for d in range(3)]
        distance = jnp.sqrt(
            delta[0] * delta[0] + delta[1] * delta[1] + delta[2] * delta[2] + SOFTENING
        )
        normal = [one_delta / distance for one_delta in delta]
        both = own_found[6] + far_found[6]
        overlap = (both - distance) / SOFT_WIDTH
        stiff = SPRING * own_found[6] * far_found[6] / both
        closing = sum((own_found[3 + d] - far_found[3 + d]) * normal[d] for d in range(3))
        soft = jnp.maximum(overlap, 0.0) + jnp.log1p(jnp.exp(-jnp.abs(overlap)))
        number = group * 1024 + sub * 128 + lane
        magnitude = jnp.where(
            number < live_count[0], stiff * (SOFT_WIDTH * soft - DAMPING * closing), 0.0
        )
        force = [magnitude * normal[d] for d in range(3)]
        values = force + [
            force[0] * normal[0],
            force[1] * normal[1],
            force[2] * normal[2],
            force[0] * normal[1],
            force[0] * normal[2],
            force[1] * normal[2],
        ]
        for k in range(9):
            high = values[k].astype(BF16).astype(F32)
            rows[pl.ds(k * 16, 8), :] = high
            rows[pl.ds(k * 16 + 8, 8), :] = values[k] - high
        for s in range(8):
            at = pl.ds(pl.multiple_of((group * 8 + s) * 128, 128), 128)
            mine = spread(own_row[s : s + 1]) == sub
            mine2 = jnp.concatenate([mine, mine], axis=0)
            hot[:, at] = hot_rows(own_c[s : s + 1])
            for k in range(9):
                high = spread(rows[pl.ds(k * 16 + s, 1), :])
                low = spread(rows[pl.ds(k * 16 + 8 + s, 1), :])
                pair = jnp.concatenate(
                    [jnp.where(mine, high, 0.0), jnp.where(mine, low, 0.0)], axis=0
                )
                lhs[k * 16 : k * 16 + 16, at] = pair.astype(BF16)
        return carry

    lax.fori_loop(0, 6, one_group, 0)
    sums = scatter_dot(lhs[...], hot[...])
    for k in range(9):
        out[k] = sums[k * 16 : k * 16 + 8] + sums[k * 16 + 8 : k * 16 + 16]


def grain_kernel(back, grain, contact, radius_ref, force_out, stress_out, lhs, hot):
    sub = subs()
    for peer in range(16):
        index = grain[pl.ds(peer, 1), :]
        mine = spread(index >> 7) == sub
        hot[:, peer * 128 : peer * 128 + 128] = hot_rows(index & 127)
        for d in range(3):
            value = jnp.where(mine, spread(back[peer, pl.ds(d, 1), :]), 0.0)
            lhs[d * 16 : d * 16 + 16, peer * 128 : peer * 128 + 128] = split_rows(value).astype(BF16)
    sums = scatter_dot(lhs[...], hot[...])
    radius = radius_ref[...]
    volume = VOLUME_FACTOR * radius * radius * radius
    for d in range(3):
        value = contact[d] + (sums[d * 16 : d * 16 + 8] + sums[d * 16 + 8 : d * 16 + 16])
        if d == 2:
            value = value - GRAIN_WEIGHT * volume
        force_out[pl.ds(d * 8, 8), :] = value
    scale = radius / volume
    for k in range(6):
        stress_out[pl.ds(k * 8, 8), :] = -contact[3 + k] * scale


def along_y(value, step):
    count = lax.axis_size("gy")
    pairs = [(i, i + step) for i in range(count) if 0 <= i + step < count]
    return lax.ppermute(value, "gy", pairs)


def along_x(value, step):
    count = lax.axis_size("gx")
    return lax.ppermute(value, "gx", [(i, (i + step) % count) for i in range(count)])


def body(
    sph_pos,
    sph_vel,
    sph_mass,
    cell_count,
    grain_pos,
    grain_vel,
    grain_radius,
    contact_pairs,
    contact_count,
    iface_grain,
    iface_offset,
    pair_count,
    iface_cell,
):
    place = jnp.stack(
        [lax.axis_index("gx"), lax.axis_index("gy"), lax.axis_index("gz")]
    ).astype(jnp.int32)
    radius = grain_radius.reshape(8, 128)
    route_grain = iface_grain.reshape(16, 128)
    send, own = call(
        pack_kernel,
        [shape(256, 128), shape(Y_TILES, 8, 128)],
        ins=[S, S] + [V] * 9,
        cost=cost(3),
    )(
        place,
        pair_count.reshape(16),
        sph_pos.reshape(96, 128),
        sph_vel.reshape(96, 128),
        sph_mass.reshape(32, 128),
        cell_count.reshape(4, 128),
        grain_pos.reshape(24, 128),
        grain_vel.reshape(24, 128),
        radius,
        route_grain,
        iface_offset.reshape(48, 128),
    )
    arrived = lax.all_to_all(
        send.reshape(16, 16, 128), "gz", split_axis=0, concat_axis=0, tiled=True
    ).reshape(256, 128)
    own = call(
        rim_kernel,
        shape(Y_TILES, 8, 128),
        ins=[S, V, pl.BlockSpec(memory_space=pl.ANY)],
        alias={2: 0},
        grid=(2,),
        out_specs=[pl.BlockSpec((1, 8, 128), lambda i: (Y_RIM + i, 0, 0))],
        cost=cost(1),
    )(place, arrived, own)
    ahead = along_y(own, 1)
    behind = along_y(own, -1)
    up, down = call(
        widen_kernel,
        [shape(X_TILES, 8, 128)] * 2,
        ins=[V] * 3,
        cost=cost(1),
    )(own, ahead, behind)
    left = along_x(up, 1)
    right = along_x(down, -1)
    fields = call(
        density_kernel,
        shape(27, 8, 128),
        ins=[S] + [V] * 5,
        scratch=[pltpu.VMEM((33 * 12, 8, 128), F32), pltpu.SMEM((81,), jnp.int32)],
        cost=cost(6),
    )(place, own, ahead, behind, left, right)
    fields_left = along_x(fields, 1)
    fields_right = along_x(fields, -1)
    send_back, reaction = call(
        pair_kernel,
        [shape(16, 4, 128), shape(12, 8, 128)],
        ins=[V] * 4,
        scratch=[pltpu.VMEM((192, 2048), BF16), pltpu.VMEM((128, 2048), BF16)],
        cost=cost(3),
    )(own, fields, arrived, iface_cell.reshape(16, 128))
    back = lax.all_to_all(send_back, "gz", split_axis=0, concat_axis=0, tiled=True)
    contact = call(
        contact_kernel,
        shape(9, 8, 128),
        ins=[S, S] + [V] * 7,
        scratch=[
            pltpu.VMEM((224, 128), F32),
            pltpu.VMEM((128, 128), F32),
            pltpu.VMEM((2, 128, 128), F32),
            pltpu.VMEM((144, 128), F32),
            pltpu.VMEM((144, 6144), BF16),
            pltpu.VMEM((128, 6144), BF16),
        ],
        cost=cost(6),
    )(
        place,
        contact_count.reshape(1),
        own,
        ahead,
        behind,
        left,
        right,
        contact_pairs[0].reshape(48, 128),
        contact_pairs[1].reshape(48, 128),
    )
    accel = call(
        force_kernel,
        shape(96, 128),
        ins=[S] + [V] * 9,
        scratch=[pltpu.VMEM((16 * 27, 8, 128), F32)],
        cost=cost(6),
    )(place, own, ahead, behind, left, right, fields, fields_left, fields_right, reaction)
    grain_force, grain_stress = call(
        grain_kernel,
        [shape(24, 128), shape(48, 128)],
        ins=[V] * 4,
        scratch=[pltpu.VMEM((48, 2048), BF16), pltpu.VMEM((128, 2048), BF16)],
        cost=cost(2),
    )(back, route_grain, contact, radius)
    return (
        accel.reshape(sph_pos.shape),
        grain_force.reshape(grain_pos.shape),
        grain_stress.reshape((6,) + grain_radius.shape),
    )


def solution(mesh):
    return jax.shard_map(
        body,
        mesh=mesh,
        in_specs=(
            P(None, None, "gx", "gy", "gz"),
            P(None, None, "gx", "gy", "gz"),
            P(None, "gx", "gy", "gz"),
            P("gx", "gy", "gz"),
            P(None, None, "gx", "gy", "gz"),
            P(None, None, "gx", "gy", "gz"),
            P(None, "gx", "gy", "gz"),
            P(None, "gx", "gy", "gz"),
            P("gx", "gy", "gz"),
            P("gx", "gy", "gz", None),
            P(None, "gx", "gy", "gz", None),
            P("gx", "gy", "gz"),
            P("gx", "gy", "gz", None),
        ),
        out_specs=(
            P(None, None, "gx", "gy", "gz"),
            P(None, None, "gx", "gy", "gz"),
            P(None, None, "gx", "gy", "gz"),
        ),
        check_vma=False,
    )
```

profile of v0, /device:TPU:6, one launch (start us, length us, event | category | flops | bytes accessed | tf_op | source)
XLA Modules:
  0.0 83.1 jit_solution(10197383155290977050)
XLA Ops:
  0.6 0.1 pad_add_fusion.place
  0.7 0.6 copy-done.3
  1.4 0.1 copy-done.2
  1.4 0.0 copy-done.4
  1.4 0.0 copy-done.9
  1.4 0.8 copy-done
  2.2 0.8 copy-done.1
  3.0 0.7 copy-done.5
  3.8 0.7 copy-done.6
  4.5 0.7 copy-done.7
  5.2 0.8 shard_map.148
  6.0 29.7 %all_to_all.10 = f32[16,16,128]{2,1,0:T(8,128)S(1)} all-to-all(f32[16,16,128]{2,1,0:T(8,128)S(1)} %bitcast.25), channel_id=1, replica_groups=mesh['gx'=8,'gy'=4,'gz'=16] {'gz'}, dimensions={0} | all-to-all | bytes 262144 | tf_op jit(solution)/shard_map/all_to_all | solution.py:669
  35.7 0.6 shard_map.149.own
  36.3 2.7 %collective-permute-start.1 = (f32[37,8,128]{2,1,0:T(8,128)S(1)}, f32[37,8,128]{2,1,0:T(8,128)S(1)}, u32[]{:S(2)}, u32[]{:S(2)}) collective-permute-start(f32[37,8,128]{2,1,0:T(8,128)S(1)} %shard_map.149.own), channel_id=1, source_target_pairs={{16,0},{32,16},{48,32},{17,1},{33,17},{49,33},{18,2},{34,18},{50,3... | collective-permute-start | bytes 454664 | tf_op jit(solution)/shard_map/ppermute | solution.py:623
  39.0 1.3 %collective-permute-start = (f32[37,8,128]{2,1,0:T(8,128)S(1)}, f32[37,8,128]{2,1,0:T(8,128)S(1)}, u32[]{:S(2)}, u32[]{:S(2)}) collective-permute-start(f32[37,8,128]{2,1,0:T(8,128)S(1)} %shard_map.149.own), channel_id=1, source_target_pairs={{0,16},{16,32},{32,48},{1,17},{17,33},{33,49},{2,18},{18,34},{34,5... | collective-permute-start | bytes 454664 | tf_op jit(solution)/shard_map/ppermute | solution.py:623
  40.3 1.4 %collective-permute-done.1.behind = f32[37,8,128]{2,1,0:T(8,128)S(1)} collective-permute-done((f32[37,8,128]{2,1,0:T(8,128)S(1)}, f32[37,8,128]{2,1,0:T(8,128)S(1)}, u32[]{:S(2)}, u32[]{:S(2)}) %collective-permute-start.1) | collective-permute-done | bytes 151584 | tf_op jit(solution)/shard_map/ppermute | solution.py:623
  41.7 4.4 %collective-permute-done.ahead = f32[37,8,128]{2,1,0:T(8,128)S(1)} collective-permute-done((f32[37,8,128]{2,1,0:T(8,128)S(1)}, f32[37,8,128]{2,1,0:T(8,128)S(1)}, u32[]{:S(2)}, u32[]{:S(2)}) %collective-permute-start) | collective-permute-done | bytes 151584 | tf_op jit(solution)/shard_map/ppermute | solution.py:623
  46.1 0.1 shard_map.150
  46.2 0.0 collective-permute-start.2
  46.2 0.0 copy-start.8
  46.2 2.9 %collective-permute-start.3 = (f32[49,8,128]{2,1,0:T(8,128)S(1)}, f32[49,8,128]{2,1,0:T(8,128)S(1)}, u32[]{:S(2)}, u32[]{:S(2)}) collective-permute-start(f32[49,8,128]{2,1,0:T(8,128)S(1)} %get-tuple-element.14), channel_id=1, source_target_pairs={{0,448},{64,0},{128,64},{192,128},{256,192},{320,256},{384,320},{4... | collective-permute-start | bytes 602120 | tf_op jit(solution)/shard_map/ppermute | solution.py:628
  49.1 3.4 %collective-permute-done.2.left = f32[49,8,128]{2,1,0:T(8,128)S(1)} collective-permute-done((f32[49,8,128]{2,1,0:T(8,128)S(1)}, f32[49,8,128]{2,1,0:T(8,128)S(1)}, u32[]{:S(2)}, u32[]{:S(2)}) %collective-permute-start.2) | collective-permute-done | bytes 200736 | tf_op jit(solution)/shard_map/ppermute | solution.py:628
  52.5 0.0 collective-permute-done.3.right
  52.5 8.3 %shard_map.151.fields = f32[27,8,128]{2,1,0:T(8,128)S(1)} custom-call(s32[3]{0:T(128)S(1)} %pad_add_fusion.place, f32[37,8,128]{2,1,0:T(8,128)S(1)} %shard_map.149.own, f32[37,8,128]{2,1,0:T(8,128)S(1)} %collective-permute-done.ahead, f32[37,8,128]{2,1,0:T(8,128)S(1)} %collective-permute-done.1.behind, f32[49,8,128]{2,1,0:T(8,128)S(1)} %collective-permute-done.2.left, ...), custom_call_target="tpu_custom_call" | custom-call | flops 24000000 | bytes 12000000 | tf_op jit(solution)/shard_map/pallas_call | solution.py:691
  60.9 3.0 %collective-permute-start.5 = (f32[27,8,128]{2,1,0:T(8,128)S(1)}, f32[27,8,128]{2,1,0:T(8,128)S(1)}, u32[]{:S(2)}, u32[]{:S(2)}) collective-permute-start(f32[27,8,128]{2,1,0:T(8,128)S(1)} %shard_map.151.fields), channel_id=1, source_target_pairs={{0,448},{64,0},{128,64},{192,128},{256,192},{320,256},{384,320},{4... | collective-permute-start | bytes 331784 | tf_op jit(solution)/shard_map/ppermute | solution.py:628
  63.8 0.0 collective-permute-start.4
  63.8 1.7 %shard_map.152 = (f32[16,4,128]{2,1,0:T(4,128)}, f32[12,8,128]{2,1,0:T(8,128)S(1)}) custom-call(f32[37,8,128]{2,1,0:T(8,128)S(1)} %shard_map.149.own, f32[27,8,128]{2,1,0:T(8,128)S(1)} %shard_map.151.fields, f32[256,128]{1,0:T(8,128)S(1)} %bitcast.24, s32[16,128]{1,0:T(8,128)S(1)} %bitcast.38), custom_call_target="tpu_custom_call" | custom-call | flops 12000000 | bytes 6000000 | tf_op jit(solution)/shard_map/pallas_call | solution.py:700
  65.5 4.0 %all-to-all-start.1 = ((f32[16,4,128]{2,1,0:T(4,128)}), f32[16,4,128]{2,1,0:T(4,128)S(1)}, u32[]{:S(2)}, u32[]{:S(2)}) async-start(f32[16,4,128]{2,1,0:T(4,128)} %get-tuple-element.16), calls=%async_computation.1 | async-start | bytes 65536 | tf_op jit(solution)/shard_map/all_to_all | solution.py:707
  70.2 4.5 %shard_map.154.contact = f32[9,8,128]{2,1,0:T(8,128)S(1)} custom-call(s32[3]{0:T(128)S(1)} %pad_add_fusion.place, s32[1]{0:T(128)} %bitcast.22.live_count, f32[37,8,128]{2,1,0:T(8,128)S(1)} %shard_map.149.own, f32[37,8,128]{2,1,0:T(8,128)S(1)} %collective-permute-done.ahead, f32[37,8,128]{2,1,0:T(8,128)S(1)} %collective-permute-done.1.behind, ...), custom_call_target="tpu_custom_call" | custom-call | flops 24000000 | bytes 12000000 | tf_op jit(solution)/shard_map/pallas_call | solution.py:708
  74.6 6.9 %shard_map.153 = f32[96,128]{1,0:T(8,128)} custom-call(s32[3]{0:T(128)S(1)} %pad_add_fusion.place, f32[37,8,128]{2,1,0:T(8,128)S(1)} %shard_map.149.own, f32[37,8,128]{2,1,0:T(8,128)S(1)} %collective-permute-done.ahead, f32[37,8,128]{2,1,0:T(8,128)S(1)} %collective-permute-done.1.behind, f32[49,8,128]{2,1,0:T(8,128)S(1)} %collective-permute-done.2.left, ...), custom_call_target="tpu_custom_call" | custom-call | flops 24000000 | bytes 12000000 | tf_op jit(solution)/shard_map/pallas_call | solution.py:732
  81.5 0.6 all-to-all-done.1.back
  82.1 1.0 %shard_map.155 = (f32[24,128]{1,0:T(8,128)}, f32[48,128]{1,0:T(8,128)}) custom-call(f32[16,4,128]{2,1,0:T(4,128)S(1)} %all-to-all-done.1.back, s32[16,128]{1,0:T(8,128)S(1)} %bitcast.31, f32[9,8,128]{2,1,0:T(8,128)S(1)} %shard_map.154.contact, f32[8,128]{1,0:T(8,128)S(1)} %bitcast.34), custom_call_target="tpu_custom_call" | custom-call | flops 8000000 | bytes 4000000 | tf_op jit(solution)/shard_map/pallas_call | solution.py:739
  (17 shorter events, 0.0 us)
Async XLA Ops:
  0.6 0.7 copy-start.3
  0.7 0.7 copy-start.2
  0.7 0.7 copy-start.4
  0.7 0.7 copy-start.9
  0.7 0.7 copy-start.10
  1.4 0.8 copy-start
  2.2 0.8 copy-start.1
  3.0 0.7 copy-start.5
  3.8 0.7 copy-start.6
  4.5 0.7 copy-start.7
  36.3 5.4 %collective-permute-start.1 = (f32[37,8,128]{2,1,0:T(8,128)S(1)}, f32[37,8,128]{2,1,0:T(8,128)S(1)}, u32[]{:S(2)}, u32[]{:S(2)}) collective-permute-start(f32[37,8,128]{2,1,0:T(8,128)S(1)} %shard_map.149.own), channel_id=1, source_target_pairs={{16,0},{32,16},{48,32},{17,1},{33,17},{49,33},{18,2},{34,18},{50,3... | collective-permute-start | bytes 454664 | tf_op jit(solution)/shard_map/ppermute | solution.py:623
  39.0 7.1 %collective-permute-start = (f32[37,8,128]{2,1,0:T(8,128)S(1)}, f32[37,8,128]{2,1,0:T(8,128)S(1)}, u32[]{:S(2)}, u32[]{:S(2)}) collective-permute-start(f32[37,8,128]{2,1,0:T(8,128)S(1)} %shard_map.149.own), channel_id=1, source_target_pairs={{0,16},{16,32},{32,48},{1,17},{17,33},{33,49},{2,18},{18,34},{34,5... | collective-permute-start | bytes 454664 | tf_op jit(solution)/shard_map/ppermute | solution.py:623
  46.2 6.4 %collective-permute-start.2 = (f32[49,8,128]{2,1,0:T(8,128)S(1)}, f32[49,8,128]{2,1,0:T(8,128)S(1)}, u32[]{:S(2)}, u32[]{:S(2)}) collective-permute-start(f32[49,8,128]{2,1,0:T(8,128)S(1)} %get-tuple-element.13), channel_id=1, source_target_pairs={{0,64},{64,128},{128,192},{192,256},{256,320},{320,384},{384,448},... | collective-permute-start | bytes 602120 | tf_op jit(solution)/shard_map/ppermute | solution.py:628
  46.2 17.6 %copy-start.8 = (s32[1,1,16,128]{3,2,1,0:T(8,128)S(1)}, s32[1,1,16,128]{3,2,1,0:T(8,128)}, u32[]{:S(2)}) copy-start(s32[1,1,16,128]{3,2,1,0:T(8,128)} %param.25) | copy-start | bytes 24580
  46.2 6.3 %collective-permute-start.3 = (f32[49,8,128]{2,1,0:T(8,128)S(1)}, f32[49,8,128]{2,1,0:T(8,128)S(1)}, u32[]{:S(2)}, u32[]{:S(2)}) collective-permute-start(f32[49,8,128]{2,1,0:T(8,128)S(1)} %get-tuple-element.14), channel_id=1, source_target_pairs={{0,448},{64,0},{128,64},{192,128},{256,192},{320,256},{384,320},{4... | collective-permute-start | bytes 602120 | tf_op jit(solution)/shard_map/ppermute | solution.py:628
  60.9 13.7 %collective-permute-start.5 = (f32[27,8,128]{2,1,0:T(8,128)S(1)}, f32[27,8,128]{2,1,0:T(8,128)S(1)}, u32[]{:S(2)}, u32[]{:S(2)}) collective-permute-start(f32[27,8,128]{2,1,0:T(8,128)S(1)} %shard_map.151.fields), channel_id=1, source_target_pairs={{0,448},{64,0},{128,64},{192,128},{256,192},{320,256},{384,320},{4... | collective-permute-start | bytes 331784 | tf_op jit(solution)/shard_map/ppermute | solution.py:628
  63.8 10.8 %collective-permute-start.4 = (f32[27,8,128]{2,1,0:T(8,128)S(1)}, f32[27,8,128]{2,1,0:T(8,128)S(1)}, u32[]{:S(2)}, u32[]{:S(2)}) collective-permute-start(f32[27,8,128]{2,1,0:T(8,128)S(1)} %shard_map.151.fields), channel_id=1, source_target_pairs={{0,64},{64,128},{128,192},{192,256},{256,320},{320,384},{384,448},... | collective-permute-start | bytes 331784 | tf_op jit(solution)/shard_map/ppermute | solution.py:628
  65.5 4.0 %copy-start.11 = (s32[2,1,1,6144]{3,2,1,0:T(1,128)S(1)}, s32[2,1,1,6144]{3,2,1,0:T(1,128)}, u32[]{:S(2)}) copy-start(s32[2,1,1,6144]{3,2,1,0:T(1,128)} %param.20) | copy-start | bytes 147460
  65.5 16.6 %all-to-all-start.1 = ((f32[16,4,128]{2,1,0:T(4,128)}), f32[16,4,128]{2,1,0:T(4,128)S(1)}, u32[]{:S(2)}, u32[]{:S(2)}) async-start(f32[16,4,128]{2,1,0:T(4,128)} %get-tuple-element.16), calls=%async_computation.1 | async-start | bytes 65536 | tf_op jit(solution)/shard_map/all_to_all | solution.py:707
where the time goes:
time: 83.7 us; the launch traced here: 83.1 us
  blocking collectives  29.7 us (35%)
  Pallas kernels  23.8 us (28%)
  starting transfers between devices  13.9 us (17%)
  waiting for transfers between devices  9.74 us (12%)
  local copies, waits for them, and re-layouts  4.45 us (5%)
  between operations  1.42 us (2%)
    all_to_all x1, blocking collectives, body(): lax.all_to_all(send.reshape(16, 16, 128), 'gz', split_axis=0, concat_axis...  29.7 us
    pallas_call x1, Pallas kernels, body(): call(density_kernel, shape(27, 8, 128), ins=[S] + [V] * 5, scratch=[pltpu...  8.33 us
    pallas_call x1, Pallas kernels, body(): call(force_kernel, shape(96, 128), ins=[S] + [V] * 9, scratch=[pltpu.VMEM...  6.91 us
    ppermute x4, starting transfers between devices, along_x(): lax.ppermute(value, 'gx', [(i, (i + step) % count) for i in range(count)])  5.92 us
    ppermute x2, waiting for transfers between devices, along_y(): return lax.ppermute(value, 'gy', pairs)  5.78 us
    pallas_call x1, Pallas kernels, body(): call(contact_kernel, shape(9, 8, 128), ins=[S, S] + [V] * 7, scratch=[plt...  4.46 us
    unnamed x24, local copies, waits for them, and re-layouts  4.45 us
    ppermute x2, starting transfers between devices, along_y(): return lax.ppermute(value, 'gy', pairs)  4.03 us
  transfers between devices with their start and end apart: 7, of which 4 were waited for; matrix products, arithmetic and copies ran while one was open for 0% of the time, Pallas kernels for 16%

commit v1 on v0

--- a/solution.py
+++ b/solution.py
@@ -34,7 +34,7 @@
 GRAIN_LANE = 56
 
 
-def call(kernel, outs, scratch=(), ins=(), cost=None, alias=None, grid=None, out_specs=None):
+def call(kernel, outs, scratch=(), ins=(), cost=None, alias=None, grid=None, out_specs=None, limit=24):
     single = not isinstance(outs, (list, tuple))
     count = 1 if single else len(outs)
     if out_specs is None:
@@ -42,6 +42,8 @@
     extra = {}
     if grid is not None:
         extra["grid"] = grid
+    if limit is not None:
+        extra["compiler_params"] = pltpu.CompilerParams(vmem_limit_bytes=limit * 1024 * 1024)
     return pl.pallas_call(
         kernel,
         out_shape=outs,
@@ -49,7 +51,6 @@
         out_specs=out_specs[0] if single else out_specs,
         scratch_shapes=list(scratch),
         input_output_aliases=alias or {},
-        compiler_params=pltpu.CompilerParams(vmem_limit_bytes=24 * 1024 * 1024),
         cost_estimate=cost,
         **extra,
     )
@@ -121,7 +122,17 @@
     return jnp.where(ids == jnp.broadcast_to(row, (128, 128)), 1.0, 0.0).astype(BF16)
 
 
-def pack_kernel(place, counts, pos, vel, mass, count, gpos, gvel, grad, grain, offset, send, own):
+def pack_kernel(place, counts, *refs):
+    sources, (send, own), buffers, sems = refs[:9], refs[9:11], refs[11:20], refs[20]
+    copies = [
+        pltpu.make_async_copy(source, buffer, sems.at[k])
+        for k, (source, buffer) in enumerate(zip(sources, buffers))
+    ]
+    for one in copies:
+        one.start()
+    for one in copies:
+        one.wait()
+    pos, vel, mass, count, gpos, gvel, grad, grain, offset = buffers
     lane = lanes()
     sub = subs()
     low = jnp.zeros((8, 128), F32)
@@ -169,14 +180,17 @@
             alive = jnp.where(sub == peer, counts[group * 8 + peer], alive)
         found[3] = jnp.where(lane < alive, found[3], 0.0)
         for field in range(3):
-            send[pl.ds(group * 128 + field, 8, stride=16), :] = offset[
+            send[pl.ds(group * 96 + field, 8, stride=12), :] = offset[
                 pl.ds(field * 16 + group * 8, 8), :
             ]
         for field in range(4):
-            send[pl.ds(group * 128 + 3 + field, 8, stride=16), :] = found[field]
-        send[pl.ds(group * 128 + 7, 8, stride=16), :] = jnp.zeros((8, 128), F32)
+            send[pl.ds(group * 96 + 3 + field, 8, stride=12), :] = found[field]
+        send[pl.ds(group * 96 + 7, 8, stride=12), :] = jnp.zeros((8, 128), F32)
+    low, high = [
+        jnp.where(lane < 64, one, pltpu.roll(roll(one, 64), 4, 0))[0:4] for one in (low, high)
+    ]
     for peer in range(16):
-        send[pl.ds(peer * 16 + 8, 8), :] = jnp.where(peer < place[2], low, high)
+        send[pl.ds(peer * 12 + 8, 4), :] = jnp.where(peer < place[2], low, high)
 
 
 def rim_kernel(place, arrived, own_in, own):
@@ -184,8 +198,8 @@
     layer = place[2]
     other = jnp.where(step == 0, layer - 1, layer + 1)
     inside = jnp.logical_and(other >= 0, other <= 15)
-    start = pl.multiple_of(jnp.clip(other, 0, 15) * 16 + 8, 8)
-    own[0] = jnp.where(inside, arrived[pl.ds(start, 8), :], 0.0)
+    rows = jnp.where(inside, arrived[jnp.clip(other, 0, 15) * 3 + 2], 0.0)
+    own[0] = jnp.concatenate([rows, pltpu.roll(rows, 64, 1)], axis=0)
 
 
 def widen_kernel(own, ahead, behind, up, down):
@@ -215,9 +229,6 @@
         self.own, self.ahead, self.behind = own, ahead, behind
         self.left, self.right = left, right
 
-    def part(self, y):
-        return (1, 0, 2)[y // 2] if y // 2 != 1 else 0
-
     def main(self, field, x, y):
         if x in (1, 2):
             source = (self.ahead, self.own, self.behind)[y // 2]
@@ -238,70 +249,82 @@
         return (1, 0, 1, 0)[x] * 2 + y % 2
 
 
-def density_kernel(place, own, ahead, behind, left, right, out, near, table):
-    lane = lanes()
-    first = lane == 0
-    last = lane == 127
-    data = Near(own, ahead, behind, left, right)
-    has_left = place[0] > 0
-    has_right = place[0] < 7
-    sign = jnp.where(lane < 64, -1.0, 1.0)
-    packed = [[jnp.zeros((8, 128), F32) for _ in range(4)] for _ in range(3)]
-    for x in range(4):
-        for y in range(6):
-            col = data.rim_col(x, y)
-            rims = [data.rim(side, x, y) for side in range(2)]
+class Columns:
+    def __init__(self, data, near, has_left=None, has_right=None):
+        self.data, self.near = data, near
+        self.there = {0: has_left, 3: has_right}
+        self.lane = lanes()
+        self.packed = None
+
+    def open_rim(self):
+        self.packed = [[jnp.zeros((8, 128), F32) for _ in range(4)] for _ in range(3)]
+
+    def put(self, at, x, y, rim):
+        data, lane, packed = self.data, self.lane, self.packed
+        col = data.rim_col(x, y)
+        rims = [data.rim(side, x, y) for side in range(2)]
+        for field in range(4):
+            value = data.main(field, x, y)
+            edge = [rims[0], rims[1]]
+            if field == 3 and x in (0, 3):
+                value = jnp.where(self.there[x], value, 0.0)
+                edge = [jnp.where(self.there[x], one, 0.0) for one in edge]
+            shift = float(x - 1) if field == 0 else float(y - 2) if field == 1 else 0.0
+            if shift:
+                value = value + shift
+                edge = [one + shift for one in edge]
+            back = jnp.where(
+                lane == 0, roll(edge[0], -rim_lane(field, 1, col)), roll(value, 1)
+            )
+            fore = jnp.where(
+                lane == 127, roll(edge[1], 127 - rim_lane(field, 0, col)), roll(value, 127)
+            )
+            if field == 2:
+                back = back - 1.0
+                fore = fore + 1.0
+            self.near[at * 12 + field] = back
+            self.near[at * 12 + 4 + field] = value
+            self.near[at * 12 + 8 + field] = fore
+            if not rim:
+                continue
+            for side in range(2):
+                spot = side * 64 + x * 8 + y
+                here = lane == spot
+                outer = rim_lane(field, 0 if side == 0 else 1, col)
+                inner = rim_lane(field, 1 if side == 0 else 0, col)
+                packed[0][field] = jnp.where(here, roll(edge[side], spot - outer), packed[0][field])
+                packed[1][field] = jnp.where(here, roll(edge[side], spot - inner), packed[1][field])
+                packed[2][field] = jnp.where(
+                    here, roll(value, spot - (0 if side == 0 else 127)), packed[2][field]
+                )
+
+    def close_rim(self):
+        sign = jnp.where(self.lane < 64, -1.0, 1.0)
+        self.packed[0][2] = self.packed[0][2] + sign
+        self.packed[2][2] = self.packed[2][2] - sign
+
+    def put_rim(self, at, moved):
+        for level in range(3):
             for field in range(4):
-                value = data.main(field, x, y)
-                edge = [rims[0], rims[1]]
-                if field == 3 and x in (0, 3):
-                    there = has_left if x == 0 else has_right
-                    value = jnp.where(there, value, 0.0)
-                    edge = [jnp.where(there, one, 0.0) for one in edge]
-                shift = float(x - 1) if field == 0 else float(y - 2) if field == 1 else 0.0
-                if shift:
-                    value = value + shift
-                    edge = [one + shift for one in edge]
-                back = jnp.where(first, roll(edge[0], -rim_lane(field, 1, col)), roll(value, 1))
-                fore = jnp.where(last, roll(edge[1], 127 - rim_lane(field, 0, col)), roll(value, 127))
-                if field == 2:
-                    back = back - 1.0
-                    fore = fore + 1.0
-                at = (x * 6 + y) * 12 + field
-                near[at] = back
-                near[at + 4] = value
-                near[at + 8] = fore
-                for side in range(2):
-                    spot = side * 64 + x * 8 + y
-                    here = lane == spot
-                    outer = rim_lane(field, 0 if side == 0 else 1, col)
-                    inner = rim_lane(field, 1 if side == 0 else 0, col)
-                    packed[0][field] = jnp.where(here, roll(edge[side], spot - outer), packed[0][field])
-                    packed[1][field] = jnp.where(here, roll(edge[side], spot - inner), packed[1][field])
-                    packed[2][field] = jnp.where(
-                        here, roll(value, spot - (0 if side == 0 else 127)), packed[2][field]
-                    )
-    packed[0][2] = packed[0][2] + sign
-    packed[2][2] = packed[2][2] - sign
-    for step_x in range(3):
-        for step_y in range(3):
-            for level in range(3):
-                for field in range(4):
-                    at = (24 + step_x * 3 + step_y) * 12 + level * 4 + field
-                    near[at] = roll(packed[level][field], -((step_x - 1) * 8 + step_y - 1))
-    for x in range(2):
-        for y in range(4):
-            for step in range(9):
-                table[(x * 4 + y) * 9 + step] = (x + step // 3) * 6 + y + step % 3
-    for step in range(9):
-        table[72 + step] = 24 + step
-
-    def one_column(target, carry):
-        middle = table[target * 9 + 4] * 12
-        center = [near[middle + 4 + field] for field in range(4)]
+                self.near[at * 12 + level * 4 + field] = moved(self.packed[level][field])
+
+
+def place_of(data, x, y):
+    value = [data.main(field, x, y) for field in range(4)]
+    if x != 1:
+        value[0] = value[0] + float(x - 1)
+    if y != 2:
+        value[1] = value[1] + float(y - 2)
+    return value
+
+
+def add_columns(near, table, start, targets, width, center_ref, total_ref):
+    def one_column(number, carry):
+        target = table[start + number * (width + 1)]
+        center = [center_ref[target * 4 + field] for field in range(3)]
 
         def one_neighbour(step, total):
-            base = table[target * 9 + step] * 12
+            base = table[start + number * (width + 1) + 1 + step] * 12
             for level in range(3):
                 for slot in range(8):
                     row = [
@@ -314,22 +337,151 @@
                     square = jnp.maximum(dx * dx + dy * dy + dz * dz, TINY)
                     radius = square * lax.rsqrt(square)
                     reach = jnp.maximum(1.0 - radius, 0.0)
-                    reach = reach * reach
-                    total = total + (reach * reach) * (4.0 * radius + 1.0) * row[3]
+                    squared = reach * reach
+                    total = total + (squared * squared) * ((1.25 - reach) * row[3])
             return total
 
-        total = lax.fori_loop(0, 9, one_neighbour, jnp.zeros((8, 128), F32))
-        density = NORMING * total
-        alive = center[3] > 0.0
-        live = jnp.where(alive, 1.0, 0.0)
-        safe = jnp.where(alive, density, 1.0)
-        pressure = (density - REST_DENSITY) * live
-        out[target * 3] = pressure / (safe * safe)
-        out[target * 3 + 1] = live / safe
-        out[target * 3 + 2] = pressure
+        total_ref[target] = lax.fori_loop(0, width, one_neighbour, total_ref[target])
         return carry
 
-    lax.fori_loop(0, 9, one_column, 0)
+    lax.fori_loop(0, targets, one_column, 0)
+
+
+def fill(table, start, rows):
+    at = start
+    for row in rows:
+        for value in row:
+            table[at] = value
+            at += 1
+    return at
+
+
+def own_density_kernel(own, total, near, center, table):
+    data = Near(own, own, own, own, own)
+    cols = Columns(data, near)
+    rows = []
+    for x in range(2):
+        for y in range(2):
+            cols.put(x * 2 + y, x + 1, y + 2, False)
+            target = x * 4 + y + 1
+            rows.append([target, 0, 1, 2, 3])
+            for field, value in enumerate(place_of(data, x + 1, y + 2)):
+                center[target * 4 + field] = value
+    fill(table, 0, rows)
+    total[...] = jnp.zeros((9, 8, 128), F32)
+    add_columns(near, table, 0, 4, 4, center, total)
+
+
+def mid_density_kernel(own, ahead, behind, start, total, rim_center, near, center, table):
+    data = Near(own, ahead, behind, own, own)
+    cols = Columns(data, near)
+    cols.open_rim()
+    for x in range(2):
+        for y in range(6):
+            cols.put(x * 6 + y, x + 1, y, True)
+    cols.close_rim()
+    lane = lanes()
+    in_first = (lane & 63) < 16
+    for step in range(3):
+        cols.put_rim(12 + step, lambda v: roll(v, 1 - step))
+        cols.put_rim(
+            15 + step,
+            lambda v: jnp.where(in_first, roll(v, 1 - step - 8), roll(v, 1 - step + 8)),
+        )
+    for field in range(4):
+        center[8 * 4 + field] = cols.packed[1][field]
+        rim_center[field] = cols.packed[1][field]
+    outer, inner = [], []
+    for x in range(2):
+        for y in range(4):
+            target = x * 4 + y
+            for field, value in enumerate(place_of(data, x + 1, y + 1)):
+                center[target * 4 + field] = value
+            if y in (0, 3):
+                outer.append([target] + [sx * 6 + y + dy for sx in range(2) for dy in range(3)])
+            else:
+                far = 1 if y == 1 else 4
+                inner.append([target] + [sx * 6 + far for sx in range(2)])
+    outer.append([8] + [12 + k for k in range(6)])
+    total[...] = start[...]
+    at = fill(table, 0, outer)
+    fill(table, at, inner)
+    add_columns(near, table, 0, 5, 6, center, total)
+    add_columns(near, table, at, 4, 2, center, total)
+
+
+def far_own_kernel(place, own, ahead, behind, left, right, start, out, near, center, table, total):
+    data = Near(own, ahead, behind, left, right)
+    cols = Columns(data, near, place[0] > 0, place[0] < 7)
+    for x in range(2):
+        for y in range(4):
+            cols.put(x * 4 + y, x * 3, y + 1, False)
+    rows = []
+    for x in range(2):
+        for y in (1, 2):
+            target = x * 4 + y
+            for field, value in enumerate(place_of(data, x + 1, y + 1)):
+                center[target * 4 + field] = value
+            rows.append([target] + [x * 4 + y - 1 + dy for dy in range(3)])
+            total[target] = start[target]
+    fill(table, 0, rows)
+    add_columns(near, table, 0, 4, 3, center, total)
+    for x in range(2):
+        for y in (1, 2):
+            press, inverse, pressure = finish(total[x * 4 + y], center[(x * 4 + y) * 4 + 3])
+            at = (x * 2 + y - 1) * 3
+            out[at] = press
+            out[at + 1] = inverse
+            out[at + 2] = pressure
+
+
+def far_rest_kernel(
+    place, own, ahead, behind, left, right, start, rim_center, own_fields, out, near, center, table, total
+):
+    data = Near(own, ahead, behind, left, right)
+    cols = Columns(data, near, place[0] > 0, place[0] < 7)
+    cols.open_rim()
+    for x in range(2):
+        for y in range(6):
+            cols.put(x * 6 + y, x * 3, y, True)
+    cols.close_rim()
+    in_first = (lanes() & 63) < 16
+    for step in range(3):
+        cols.put_rim(
+            12 + step,
+            lambda v: jnp.where(in_first, roll(v, 1 - step + 8), roll(v, 1 - step - 8)),
+        )
+    rows = []
+    for x in range(2):
+        for y in (0, 3):
+            target = x * 4 + y
+            for field, value in enumerate(place_of(data, x + 1, y + 1)):
+                center[target * 4 + field] = value
+            rows.append([target] + [x * 6 + y + dy for dy in range(3)])
+            total[target] = start[target]
+    for field in range(4):
+        center[8 * 4 + field] = rim_center[field]
+    total[8] = start[8]
+    rows.append([8, 12, 13, 14])
+    fill(table, 0, rows)
+    add_columns(near, table, 0, 5, 3, center, total)
+    for target in (0, 3, 4, 7, 8):
+        press, inverse, _ = finish(total[target], center[target * 4 + 3])
+        out[target * 2] = press
+        out[target * 2 + 1] = inverse
+    for x in range(2):
+        for y in range(2):
+            for k in range(2):
+                out[(x * 4 + y + 1) * 2 + k] = own_fields[(x * 2 + y) * 3 + k]
+
+
+def finish(total, mass):
+    density = (4.0 * NORMING) * total
+    alive = mass > 0.0
+    live = jnp.where(alive, 1.0, 0.0)
+    safe = jnp.where(alive, density, 1.0)
+    pressure = (density - REST_DENSITY) * live
+    return pressure / (safe * safe), live / safe, pressure
 
 
 def force_kernel(place, own, ahead, behind, left, right, fields, fleft, fright, reaction, out, near):
@@ -348,8 +500,8 @@
             target = far_x * 4 + y - 1
             extra = []
             for which in range(2):
-                value = source[target * 3 + which]
-                halo = source[24 + which]
+                value = source[target * 2 + which]
+                halo = source[16 + which]
                 extra.append((value, halo))
             levels = [[], [], []]
             for field in range(7):
@@ -386,8 +538,8 @@
         b = target % 2
         middle = (((a + 1) * 4 + b + 1) * 3 + 1) * 9
         center = [near[middle + k] for k in range(3)]
-        press = fields[(a * 4 + b + 1) * 3]
-        inverse = fields[(a * 4 + b + 1) * 3 + 1]
+        press = fields[(a * 4 + b + 1) * 2]
+        inverse = fields[(a * 4 + b + 1) * 2 + 1]
 
         def one_neighbour(step, total):
             base = (((a + step // 3) * 4 + b + step % 3) * 3) * 9
@@ -406,8 +558,8 @@
                     reach = jnp.maximum(1.0 - radius, 0.0)
                     cubed = reach * reach * reach
                     push = cubed * (row[3] * press + row[4])
-                    soft = lax.rsqrt(square + SOFTENING)
-                    drag = (cubed * row[5]) * (square * soft * soft)
+                    soft = pltpu.reciprocal(square + SOFTENING, approx=True)
+                    drag = (cubed * row[5]) * (square * soft)
                     total[0] = total[0] + push * dx
                     total[1] = total[1] + push * dy
                     total[2] = total[2] + push * dz
@@ -439,7 +591,7 @@
         col_of = spread(index >> 7)
         found = None
         for col in range(4):
-            mid = ((col // 2) * 4 + col % 2 + 1) * 3
+            mid = col * 3
             inverse = fields[mid + 1]
             tables = [own[col * 7 + k] for k in (0, 1, 2, 4, 5, 6)]
             tables += [own[col * 7 + 3] * inverse, fields[mid + 2], inverse]
@@ -449,7 +601,7 @@
             else:
                 here = col_of == col
                 found = [jnp.where(here, new, old) for new, old in zip(got, found)]
-        row = [spread(arrived[pl.ds(peer * 16 + k, 1), :]) for k in range(7)]
+        row = [spread(arrived[peer * 3 + k // 4, pl.ds(k % 4, 1), :]) for k in range(7)]
         delta = [row[d] - found[d] for d in range(3)]
         square = jnp.maximum(delta[0] * delta[0] + delta[1] * delta[1] + delta[2] * delta[2], TINY)
         radius = square * lax.rsqrt(square)
@@ -474,27 +626,20 @@
         reaction[k] = sums[k * 16 : k * 16 + 8] + sums[k * 16 + 8 : k * 16 + 16]
 
 
-def contact_kernel(place, live_count, own, ahead, behind, left, right, first, second, out, table, rims, turned, rows, lhs, hot):
+def contact_kernel(place, live_count, own, ahead, behind, left, right, listed, out, rims, turned, rows, lhs, hot):
     lane = lanes()
     sub = subs()
     has_left = place[0] > 0
     has_right = place[0] < 7
-    for field in range(7):
-        for slot in range(2):
-            for x in range(4):
-                for y in range(4):
-                    if x in (1, 2):
-                        source = (ahead, own, own, behind)[y]
-                        value = source[
-                            Y_GRAIN + field,
-                            pl.ds(slot * 4 + (x - 1) * 2 + (1, 0, 1, 0)[y], 1),
-                            :,
-                        ]
-                    else:
-                        source, there = (left, has_left) if x == 0 else (right, has_right)
-                        value = source[X_GRAIN + field, pl.ds(slot * 4 + y, 1), :]
-                        value = jnp.where(there, value, 0.0)
-                    table[pl.ds(field * 32 + slot * 16 + x * 4 + y, 1), :] = value
+    def far_line(field, row):
+        slot, x, y = row // 16, row // 4 % 4, row % 4
+        if x in (1, 2):
+            source = (ahead, own, own, behind)[y]
+            at = slot * 4 + (x - 1) * 2 + (1, 0, 1, 0)[y]
+            return source[Y_GRAIN + field, pl.ds(at, 1), :]
+        source = left if x == 0 else right
+        return source[X_GRAIN + field, pl.ds(slot * 4 + y, 1), :]
+
     for side in range(2):
         rims[...] = jnp.zeros((128, 128), F32)
         for part, source in enumerate((own, ahead, behind)):
@@ -507,10 +652,10 @@
             )
         turned[side] = jnp.transpose(rims[...])
 
-    def one_group(group, carry):
-        start = pl.multiple_of(group * 8, 8)
-        one = first[pl.ds(start, 8), :]
-        two = second[pl.ds(start, 8), :]
+    def one_group(group):
+        start = group * 8
+        one = listed[pl.ds(start, 8), :]
+        two = listed[pl.ds(start + 48, 8), :]
         own_row = one >> 7
         own_c = one & 127
         far_row = (two * 4033) >> 19
@@ -533,8 +678,10 @@
         far_found = [jnp.zeros((8, 128), F32) for _ in range(7)]
         for row in range(32):
             here = far_row == row
+            if row // 4 % 4 in (0, 3):
+                here = jnp.logical_and(here, has_left if row // 4 % 4 == 0 else has_right)
             for field in range(7):
-                got = lane_gather(spread(table[pl.ds(field * 32 + row, 1), :]), far_at)
+                got = lane_gather(spread(far_line(field, row)), far_at)
                 far_found[field] = jnp.where(here, got, far_found[field])
         for side, edge in ((0, 0), (1, 129)):
             here = far_c == edge
@@ -573,23 +720,22 @@
         ]
         for k in range(9):
             high = values[k].astype(BF16).astype(F32)
-            rows[pl.ds(k * 16, 8), :] = high
-            rows[pl.ds(k * 16 + 8, 8), :] = values[k] - high
+            rows[group, pl.ds(k * 16, 8), :] = high
+            rows[group, pl.ds(k * 16 + 8, 8), :] = values[k] - high
         for s in range(8):
-            at = pl.ds(pl.multiple_of((group * 8 + s) * 128, 128), 128)
+            at = pl.ds((group * 8 + s) * 128, 128)
             mine = spread(own_row[s : s + 1]) == sub
-            mine2 = jnp.concatenate([mine, mine], axis=0)
             hot[:, at] = hot_rows(own_c[s : s + 1])
             for k in range(9):
-                high = spread(rows[pl.ds(k * 16 + s, 1), :])
-                low = spread(rows[pl.ds(k * 16 + 8 + s, 1), :])
+                high = spread(rows[group, pl.ds(k * 16 + s, 1), :])
+                low = spread(rows[group, pl.ds(k * 16 + 8 + s, 1), :])
                 pair = jnp.concatenate(
                     [jnp.where(mine, high, 0.0), jnp.where(mine, low, 0.0)], axis=0
                 )
                 lhs[k * 16 : k * 16 + 16, at] = pair.astype(BF16)
-        return carry
-
-    lax.fori_loop(0, 6, one_group, 0)
+
+    for group in range(6):
+        one_group(group)
     sums = scatter_dot(lhs[...], hot[...])
     for k in range(9):
         out[k] = sums[k * 16 : k * 16 + 8] + sums[k * 16 + 8 : k * 16 + 16]
@@ -615,6 +761,14 @@
     scale = radius / volume
     for k in range(6):
         stress_out[pl.ds(k * 8, 8), :] = -contact[3 + k] * scale
+
+
+def density_scratch(columns):
+    return [
+        pltpu.VMEM((columns * 12, 8, 128), F32),
+        pltpu.VMEM((36, 8, 128), F32),
+        pltpu.SMEM((64,), jnp.int32),
+    ]
 
 
 def along_y(value, step):
@@ -650,9 +804,15 @@
     route_grain = iface_grain.reshape(16, 128)
     send, own = call(
         pack_kernel,
-        [shape(256, 128), shape(Y_TILES, 8, 128)],
-        ins=[S, S] + [V] * 9,
+        [shape(192, 128), shape(Y_TILES, 8, 128)],
+        ins=[S, S] + [pl.BlockSpec(memory_space=pltpu.HBM)] * 9,
+        scratch=[pltpu.VMEM((rows, 128), F32) for rows in (96, 96, 32)]
+        + [pltpu.VMEM((4, 128), jnp.int32)]
+        + [pltpu.VMEM((rows, 128), F32) for rows in (24, 24, 8)]
+        + [pltpu.VMEM((16, 128), jnp.int32), pltpu.VMEM((48, 128), F32)]
+        + [pltpu.SemaphoreType.DMA((9,))],
         cost=cost(3),
+        limit=None,
     )(
         place,
         pair_count.reshape(16),
@@ -667,8 +827,8 @@
         iface_offset.reshape(48, 128),
     )
     arrived = lax.all_to_all(
-        send.reshape(16, 16, 128), "gz", split_axis=0, concat_axis=0, tiled=True
-    ).reshape(256, 128)
+        send.reshape(16, 3, 4, 128), "gz", split_axis=0, concat_axis=0, tiled=True
+    ).reshape(48, 4, 128)
     own = call(
         rim_kernel,
         shape(Y_TILES, 8, 128),
@@ -680,6 +840,14 @@
     )(place, arrived, own)
     ahead = along_y(own, 1)
     behind = along_y(own, -1)
+    own_total = call(
+        own_density_kernel,
+        shape(9, 8, 128),
+        ins=[V],
+        scratch=density_scratch(4),
+        cost=cost(3),
+    )(own)
+    ahead, behind, own_total = lax.optimization_barrier((ahead, behind, own_total))
     up, down = call(
         widen_kernel,
         [shape(X_TILES, 8, 128)] * 2,
@@ -688,32 +856,45 @@
     )(own, ahead, behind)
     left = along_x(up, 1)
     right = along_x(down, -1)
-    fields = call(
-        density_kernel,
-        shape(27, 8, 128),
-        ins=[S] + [V] * 5,
-        scratch=[pltpu.VMEM((33 * 12, 8, 128), F32), pltpu.SMEM((81,), jnp.int32)],
+    mid_total, rim_center = call(
+        mid_density_kernel,
+        [shape(9, 8, 128), shape(4, 8, 128)],
+        ins=[V] * 4,
+        scratch=density_scratch(18),
         cost=cost(6),
-    )(place, own, ahead, behind, left, right)
-    fields_left = along_x(fields, 1)
-    fields_right = along_x(fields, -1)
+    )(own, ahead, behind, own_total)
+    own_fields = call(
+        far_own_kernel,
+        shape(12, 8, 128),
+        ins=[S] + [V] * 6,
+        scratch=density_scratch(8) + [pltpu.VMEM((9, 8, 128), F32)],
+        cost=cost(2),
+    )(place, own, ahead, behind, left, right, mid_total)
     send_back, reaction = call(
         pair_kernel,
         [shape(16, 4, 128), shape(12, 8, 128)],
         ins=[V] * 4,
         scratch=[pltpu.VMEM((192, 2048), BF16), pltpu.VMEM((128, 2048), BF16)],
         cost=cost(3),
-    )(own, fields, arrived, iface_cell.reshape(16, 128))
+    )(own, own_fields, arrived, iface_cell.reshape(16, 128))
+    fields = call(
+        far_rest_kernel,
+        shape(18, 8, 128),
+        ins=[S] + [V] * 8,
+        scratch=density_scratch(15) + [pltpu.VMEM((9, 8, 128), F32)],
+        cost=cost(3),
+    )(place, own, ahead, behind, left, right, mid_total, rim_center, own_fields)
+    fields_left = along_x(fields, 1)
+    fields_right = along_x(fields, -1)
     back = lax.all_to_all(send_back, "gz", split_axis=0, concat_axis=0, tiled=True)
     contact = call(
         contact_kernel,
         shape(9, 8, 128),
-        ins=[S, S] + [V] * 7,
+        ins=[S, S] + [V] * 6,
         scratch=[
-            pltpu.VMEM((224, 128), F32),
             pltpu.VMEM((128, 128), F32),
             pltpu.VMEM((2, 128, 128), F32),
-            pltpu.VMEM((144, 128), F32),
+            pltpu.VMEM((6, 144, 128), F32),
             pltpu.VMEM((144, 6144), BF16),
             pltpu.VMEM((128, 6144), BF16),
         ],
@@ -726,8 +907,7 @@
         behind,
         left,
         right,
-        contact_pairs[0].reshape(48, 128),
-        contact_pairs[1].reshape(48, 128),
+        contact_pairs.reshape(96, 128),
     )
     accel = call(
         force_kernel,

time: 83.7 us -> 75.8 us (0.906)
  the two profiles are of different devices: /device:TPU:6 before, /device:TPU:32 now
where the time goes in v1:
time: 75.8 us; the launch traced here: 75.4 us
  blocking collectives  28.3 us (37%)
  Pallas kernels  25.2 us (33%)
  starting transfers between devices  14.7 us (19%)
  waiting for transfers between devices  4.39 us (6%)
  between operations  1.47 us (2%)
    all_to_all x1, blocking collectives, body(): lax.all_to_all(send.reshape(16, 3, 4, 128), 'gz', split_axis=0, concat_ax...  28.3 us
    pallas_call x1, Pallas kernels, body(): call(force_kernel, shape(96, 128), ins=[S] + [V] * 9, scratch=[pltpu.VMEM...  6.85 us
    ppermute x4, starting transfers between devices, along_x(): lax.ppermute(value, 'gx', [(i, (i + step) % count) for i in range(count)])  5.92 us
    ppermute x2, starting transfers between devices, along_y(): return lax.ppermute(value, 'gy', pairs)  4.68 us
    ppermute x2, waiting for transfers between devices, along_y(): return lax.ppermute(value, 'gy', pairs)  4.38 us
    all_to_all x1, starting transfers between devices, body(): lax.all_to_all(send_back, 'gz', split_axis=0, concat_axis=0, tiled=True)  4.14 us
    pallas_call x1, Pallas kernels, body(): call(mid_density_kernel, [shape(9, 8, 128), shape(4, 8, 128)], ins=[V] *...  3.69 us
    pallas_call x1, Pallas kernels, body(): call(contact_kernel, shape(9, 8, 128), ins=[S, S] + [V] * 6, scratch=[plt...  3.18 us
  transfers between devices with their start and end apart: 7, of which 1 were waited for; matrix products, arithmetic and copies ran while one was open for 0% of the time, Pallas kernels for 23%

profile of v1, /device:TPU:32, one launch (start us, length us, event | category | flops | bytes accessed | tf_op | source)
XLA Modules:
  0.0 75.4 jit_solution(7660961345108834126)
XLA Ops:
  0.6 0.6 pad_add_fusion.place
  1.3 2.6 %shard_map.148 = (f32[192,128]{1,0:T(8,128)}, f32[37,8,128]{2,1,0:T(8,128)}) custom-call(s32[3]{0:T(128)} %pad_add_fusion.place, s32[16]{0:T(128)} %bitcast.39, f32[96,128]{1,0:T(8,128)} %bitcast.32, f32[96,128]{1,0:T(8,128)} %bitcast.33, f32[32,128]{1,0:T(8,128)} %bitcast.35, s32[4,128]{1,0:T(4,128)} %bitcast.38, f32[24,128]{1,0:T(8,128)} %bitcast.36, ...), custom_call_target="tpu_custom_call" | custom-call | flops 12000000 | bytes 6000000 | tf_op jit(solution)/shard_map/pallas_call | solution.py:805
  3.8 28.3 %all_to_all.10 = f32[16,3,4,128]{3,2,1,0:T(4,128)S(1)} all-to-all(f32[16,3,4,128]{3,2,1,0:T(4,128)} %bitcast.30), channel_id=1, replica_groups=mesh['gx'=8,'gy'=4,'gz'=16] {'gz'}, dimensions={0} | all-to-all | bytes 196608 | tf_op jit(solution)/shard_map/all_to_all | solution.py:829
  32.2 0.6 copy-done.3
  32.8 0.7 shard_map.149.own
  33.5 3.4 %collective-permute-start = (f32[37,8,128]{2,1,0:T(8,128)S(1)}, f32[37,8,128]{2,1,0:T(8,128)S(1)}, u32[]{:S(2)}, u32[]{:S(2)}) collective-permute-start(f32[37,8,128]{2,1,0:T(8,128)S(1)} %shard_map.149.own), channel_id=1, source_target_pairs={{0,16},{16,32},{32,48},{1,17},{17,33},{33,49},{2,18},{18,34},{34,5... | collective-permute-start | bytes 454664 | tf_op jit(solution)/shard_map/ppermute | solution.py:777
  36.9 1.3 %collective-permute-start.1 = (f32[37,8,128]{2,1,0:T(8,128)S(1)}, f32[37,8,128]{2,1,0:T(8,128)S(1)}, u32[]{:S(2)}, u32[]{:S(2)}) collective-permute-start(f32[37,8,128]{2,1,0:T(8,128)S(1)} %shard_map.149.own), channel_id=1, source_target_pairs={{16,0},{32,16},{48,32},{17,1},{33,17},{49,33},{18,2},{34,18},{50,3... | collective-permute-start | bytes 454664 | tf_op jit(solution)/shard_map/ppermute | solution.py:777
  38.2 1.4 %shard_map.150.start = f32[9,8,128]{2,1,0:T(8,128)S(1)} custom-call(f32[37,8,128]{2,1,0:T(8,128)S(1)} %shard_map.149.own), custom_call_target="tpu_custom_call" | custom-call | flops 12000000 | bytes 6000000 | tf_op jit(solution)/shard_map/pallas_call | solution.py:843
  39.6 0.0 collective-permute-done.ahead
  39.6 4.4 %collective-permute-done.1.behind = f32[37,8,128]{2,1,0:T(8,128)S(1)} collective-permute-done((f32[37,8,128]{2,1,0:T(8,128)S(1)}, f32[37,8,128]{2,1,0:T(8,128)S(1)}, u32[]{:S(2)}, u32[]{:S(2)}) %collective-permute-start.1) | collective-permute-done | bytes 151584 | tf_op jit(solution)/shard_map/ppermute | solution.py:777
  44.0 0.1 shard_map.151
  44.1 0.0 collective-permute-start.2
  44.1 2.9 %collective-permute-start.3 = (f32[49,8,128]{2,1,0:T(8,128)S(1)}, f32[49,8,128]{2,1,0:T(8,128)S(1)}, u32[]{:S(2)}, u32[]{:S(2)}) collective-permute-start(f32[49,8,128]{2,1,0:T(8,128)S(1)} %get-tuple-element.21), channel_id=1, source_target_pairs={{0,448},{64,0},{128,64},{192,128},{256,192},{320,256},{384,320},{4... | collective-permute-start | bytes 602120 | tf_op jit(solution)/shard_map/ppermute | solution.py:782
  47.0 3.7 %shard_map.152 = (f32[9,8,128]{2,1,0:T(8,128)S(1)}, f32[4,8,128]{2,1,0:T(8,128)S(1)}) custom-call(f32[37,8,128]{2,1,0:T(8,128)S(1)} %shard_map.149.own, f32[37,8,128]{2,1,0:T(8,128)S(1)} %collective-permute-done.ahead, f32[37,8,128]{2,1,0:T(8,128)S(1)} %collective-permute-done.1.behind, f32[9,8,128]{2,1,0:T(8,128)S(1)} %shard_map.150.start), custom_call_target="tpu_custom_call" | custom-call | flops 24000000 | bytes 12000000 | tf_op jit(solution)/shard_map/pallas_call | solution.py:859
  50.7 0.0 collective-permute-done.2.left
  50.7 0.0 collective-permute-done.3.right
  50.7 0.0 copy-start.5
  50.8 1.7 %shard_map.153.own_fields.fields = f32[12,8,128]{2,1,0:T(8,128)S(1)} custom-call(s32[3]{0:T(128)S(1)} %copy-done.3, f32[37,8,128]{2,1,0:T(8,128)S(1)} %shard_map.149.own, f32[37,8,128]{2,1,0:T(8,128)S(1)} %collective-permute-done.ahead, f32[37,8,128]{2,1,0:T(8,128)S(1)} %collective-permute-done.1.behind, f32[49,8,128]{2,1,0:T(8,128)S(1)} %collective-permute-done.2.left, ...), custom_call_target="tpu_custom_call" | custom-call | flops 8000000 | bytes 4000000 | tf_op jit(solution)/shard_map/pallas_call | solution.py:866
  52.5 1.7 %shard_map.155 = (f32[16,4,128]{2,1,0:T(4,128)}, f32[12,8,128]{2,1,0:T(8,128)S(1)}) custom-call(f32[37,8,128]{2,1,0:T(8,128)S(1)} %shard_map.149.own, f32[12,8,128]{2,1,0:T(8,128)S(1)} %shard_map.153.own_fields.fields, f32[48,4,128]{2,1,0:T(4,128)S(1)} %bitcast.23, s32[16,128]{1,0:T(8,128)S(1)} %bitcast.29), custom_call_target="tpu_custom_call" | custom-call | flops 12000000 | bytes 6000000 | tf_op jit(solution)/shard_map/pallas_call | solution.py:873
  54.1 4.1 %all-to-all-start.1 = ((f32[16,4,128]{2,1,0:T(4,128)}), f32[16,4,128]{2,1,0:T(4,128)S(1)}, u32[]{:S(2)}, u32[]{:S(2)}) async-start(f32[16,4,128]{2,1,0:T(4,128)} %get-tuple-element.26), calls=%async_computation.1 | async-start | bytes 65536 | tf_op jit(solution)/shard_map/all_to_all | solution.py:889
  58.3 2.4 %shard_map.154.fields = f32[18,8,128]{2,1,0:T(8,128)S(1)} custom-call(s32[3]{0:T(128)S(1)} %copy-done.3, f32[37,8,128]{2,1,0:T(8,128)S(1)} %shard_map.149.own, f32[37,8,128]{2,1,0:T(8,128)S(1)} %collective-permute-done.ahead, f32[37,8,128]{2,1,0:T(8,128)S(1)} %collective-permute-done.1.behind, f32[49,8,128]{2,1,0:T(8,128)S(1)} %collective-permute-done.2.left, ...), custom_call_target="tpu_custom_call" | custom-call | flops 12000000 | bytes 6000000 | tf_op jit(solution)/shard_map/pallas_call | solution.py:880
  60.7 0.0 collective-permute-start.4
  60.7 2.9 %collective-permute-start.5 = (f32[18,8,128]{2,1,0:T(8,128)S(1)}, f32[18,8,128]{2,1,0:T(8,128)S(1)}, u32[]{:S(2)}, u32[]{:S(2)}) collective-permute-start(f32[18,8,128]{2,1,0:T(8,128)S(1)} %shard_map.154.fields), channel_id=1, source_target_pairs={{0,448},{64,0},{128,64},{192,128},{256,192},{320,256},{384,320},{4... | collective-permute-start | bytes 221192 | tf_op jit(solution)/shard_map/ppermute | solution.py:782
  64.3 0.0 copy-done.1
  64.3 3.2 %shard_map.157.contact = f32[9,8,128]{2,1,0:T(8,128)S(1)} custom-call(s32[3]{0:T(128)S(1)} %copy-done.3, s32[1]{0:T(128)} %bitcast.21.live_count, f32[37,8,128]{2,1,0:T(8,128)S(1)} %shard_map.149.own, f32[37,8,128]{2,1,0:T(8,128)S(1)} %collective-permute-done.ahead, f32[37,8,128]{2,1,0:T(8,128)S(1)} %collective-permute-done.1.behind, ...), custom_call_target="tpu_custom_call" | custom-call | flops 24000000 | bytes 12000000 | tf_op jit(solution)/shard_map/pallas_call | solution.py:890
  67.5 0.0 collective-permute-done.4.fleft
  67.5 0.0 collective-permute-done.5.fright
  67.6 0.0 copy-start.2
  67.6 0.0 copy-start.4
  67.6 6.9 %shard_map.156 = f32[96,128]{1,0:T(8,128)} custom-call(s32[3]{0:T(128)S(1)} %copy-done.3, f32[37,8,128]{2,1,0:T(8,128)S(1)} %shard_map.149.own, f32[37,8,128]{2,1,0:T(8,128)S(1)} %collective-permute-done.ahead, f32[37,8,128]{2,1,0:T(8,128)S(1)} %collective-permute-done.1.behind, f32[49,8,128]{2,1,0:T(8,128)S(1)} %collective-permute-done.2.left, ...), custom_call_target="tpu_custom_call" | custom-call | flops 24000000 | bytes 12000000 | tf_op jit(solution)/shard_map/pallas_call | solution.py:912
  74.4 0.0 all-to-all-done.1.back
  74.4 1.0 %shard_map.158 = (f32[24,128]{1,0:T(8,128)}, f32[48,128]{1,0:T(8,128)}) custom-call(f32[16,4,128]{2,1,0:T(4,128)S(1)} %all-to-all-done.1.back, s32[16,128]{1,0:T(8,128)S(1)} %bitcast.26, f32[9,8,128]{2,1,0:T(8,128)S(1)} %shard_map.157.contact, f32[8,128]{1,0:T(8,128)S(1)} %bitcast.28), custom_call_target="tpu_custom_call" | custom-call | flops 8000000 | bytes 4000000 | tf_op jit(solution)/shard_map/pallas_call | solution.py:919
  (7 shorter events, 0.0 us)
Async XLA Ops:
  3.8 28.4 %copy-start = (f32[37,8,128]{2,1,0:T(8,128)S(1)}, f32[37,8,128]{2,1,0:T(8,128)}, u32[]{:S(2)}) copy-start(f32[37,8,128]{2,1,0:T(8,128)} %get-tuple-element.17.own_in) | copy-start | bytes 454660
  32.2 0.6 copy-start.3
  33.5 6.1 %collective-permute-start = (f32[37,8,128]{2,1,0:T(8,128)S(1)}, f32[37,8,128]{2,1,0:T(8,128)S(1)}, u32[]{:S(2)}, u32[]{:S(2)}) collective-permute-start(f32[37,8,128]{2,1,0:T(8,128)S(1)} %shard_map.149.own), channel_id=1, source_target_pairs={{0,16},{16,32},{32,48},{1,17},{17,33},{33,49},{2,18},{18,34},{34,5... | collective-permute-start | bytes 454664 | tf_op jit(solution)/shard_map/ppermute | solution.py:777
  36.9 7.1 %collective-permute-start.1 = (f32[37,8,128]{2,1,0:T(8,128)S(1)}, f32[37,8,128]{2,1,0:T(8,128)S(1)}, u32[]{:S(2)}, u32[]{:S(2)}) collective-permute-start(f32[37,8,128]{2,1,0:T(8,128)S(1)} %shard_map.149.own), channel_id=1, source_target_pairs={{16,0},{32,16},{48,32},{17,1},{33,17},{49,33},{18,2},{34,18},{50,3... | collective-permute-start | bytes 454664 | tf_op jit(solution)/shard_map/ppermute | solution.py:777
  44.1 6.7 %collective-permute-start.2 = (f32[49,8,128]{2,1,0:T(8,128)S(1)}, f32[49,8,128]{2,1,0:T(8,128)S(1)}, u32[]{:S(2)}, u32[]{:S(2)}) collective-permute-start(f32[49,8,128]{2,1,0:T(8,128)S(1)} %get-tuple-element.20), channel_id=1, source_target_pairs={{0,64},{64,128},{128,192},{192,256},{256,320},{320,384},{384,448},... | collective-permute-start | bytes 602120 | tf_op jit(solution)/shard_map/ppermute | solution.py:782
  44.1 6.7 %collective-permute-start.3 = (f32[49,8,128]{2,1,0:T(8,128)S(1)}, f32[49,8,128]{2,1,0:T(8,128)S(1)}, u32[]{:S(2)}, u32[]{:S(2)}) collective-permute-start(f32[49,8,128]{2,1,0:T(8,128)S(1)} %get-tuple-element.21), channel_id=1, source_target_pairs={{0,448},{64,0},{128,64},{192,128},{256,192},{320,256},{384,320},{4... | collective-permute-start | bytes 602120 | tf_op jit(solution)/shard_map/ppermute | solution.py:782
  50.7 1.7 %copy-start.5 = (s32[1,1,16,128]{3,2,1,0:T(8,128)S(1)}, s32[1,1,16,128]{3,2,1,0:T(8,128)}, u32[]{:S(2)}) copy-start(s32[1,1,16,128]{3,2,1,0:T(8,128)} %param.25) | copy-start | bytes 24580
  54.1 20.3 %all-to-all-start.1 = ((f32[16,4,128]{2,1,0:T(4,128)}), f32[16,4,128]{2,1,0:T(4,128)S(1)}, u32[]{:S(2)}, u32[]{:S(2)}) async-start(f32[16,4,128]{2,1,0:T(4,128)} %get-tuple-element.26), calls=%async_computation.1 | async-start | bytes 65536 | tf_op jit(solution)/shard_map/all_to_all | solution.py:889
  58.3 6.1 %copy-start.1 = (s32[2,1,1,6144]{3,2,1,0:T(1,128)S(1)}, s32[2,1,1,6144]{3,2,1,0:T(1,128)}, u32[]{:S(2)}) copy-start(s32[2,1,1,6144]{3,2,1,0:T(1,128)} %param.20) | copy-start | bytes 147460
  60.7 6.8 %collective-permute-start.4 = (f32[18,8,128]{2,1,0:T(8,128)S(1)}, f32[18,8,128]{2,1,0:T(8,128)S(1)}, u32[]{:S(2)}, u32[]{:S(2)}) collective-permute-start(f32[18,8,128]{2,1,0:T(8,128)S(1)} %shard_map.154.fields), channel_id=1, source_target_pairs={{0,64},{64,128},{128,192},{192,256},{256,320},{320,384},{384,448},... | collective-permute-start | bytes 221192 | tf_op jit(solution)/shard_map/ppermute | solution.py:782
  60.7 6.8 %collective-permute-start.5 = (f32[18,8,128]{2,1,0:T(8,128)S(1)}, f32[18,8,128]{2,1,0:T(8,128)S(1)}, u32[]{:S(2)}, u32[]{:S(2)}) collective-permute-start(f32[18,8,128]{2,1,0:T(8,128)S(1)} %shard_map.154.fields), channel_id=1, source_target_pairs={{0,448},{64,0},{128,64},{192,128},{256,192},{320,256},{384,320},{4... | collective-permute-start | bytes 221192 | tf_op jit(solution)/shard_map/ppermute | solution.py:782
  67.6 6.9 %copy-start.2 = (s32[1,1,16,128]{3,2,1,0:T(8,128)S(1)}, s32[1,1,16,128]{3,2,1,0:T(8,128)}, u32[]{:S(2)}) copy-start(s32[1,1,16,128]{3,2,1,0:T(8,128)} %param.22) | copy-start | bytes 24580
  67.6 6.9 %copy-start.4 = (f32[2,2,2,128]{3,2,1,0:T(2,128)S(1)}, f32[2,2,2,128]{3,2,1,0:T(2,128)}, u32[]{:S(2)}) copy-start(f32[2,2,2,128]{3,2,1,0:T(2,128)} %param.19) | copy-start | bytes 12292

commit v2 on v1

--- a/solution.py
+++ b/solution.py
@@ -122,8 +122,36 @@
     return jnp.where(ids == jnp.broadcast_to(row, (128, 128)), 1.0, 0.0).astype(BF16)
 
 
-def pack_kernel(place, counts, *refs):
-    sources, (send, own), buffers, sems = refs[:9], refs[9:11], refs[11:20], refs[20]
+def water_tile(pos, vel, mass, count, col, field):
+    if field < 3:
+        return pos[pl.ds(field * 32 + col, 8, stride=4), :]
+    if field > 3:
+        return vel[pl.ds((field - 4) * 32 + col, 8, stride=4), :]
+    value = mass[pl.ds(col, 8, stride=4), :]
+    return jnp.where(subs() < spread(count[pl.ds(col, 1), :]), value, 0.0)
+
+
+def grain_tile(gpos, gvel, grad, field):
+    if field < 3:
+        return gpos[pl.ds(field * 8, 8), :]
+    if field < 6:
+        return gvel[pl.ds((field - 3) * 8, 8), :]
+    return grad[...]
+
+
+def gather_kernel(pos, vel, mass, count, gpos, gvel, grad, own):
+    for col in range(4):
+        for field in range(7):
+            own[col * 7 + field] = water_tile(pos, vel, mass, count, col, field)
+    for field in range(7):
+        own[Y_GRAIN + field] = grain_tile(gpos, gvel, grad, field)
+    for side in range(2):
+        own[Y_RIM + side] = jnp.zeros((8, 128), F32)
+
+
+def pack_kernel(counts, *refs):
+    sources, send, buffers, sems = refs[:9], refs[9], refs[10:19], refs[19]
+    layer_here = lax.axis_index("gz")
     copies = [
         pltpu.make_async_copy(source, buffer, sems.at[k])
         for k, (source, buffer) in enumerate(zip(sources, buffers))
@@ -139,26 +167,13 @@
     high = jnp.zeros((8, 128), F32)
     for col in range(4):
         for field in range(7):
-            if field < 3:
-                value = pos[pl.ds(field * 32 + col, 8, stride=4), :]
-            elif field == 3:
-                value = mass[pl.ds(col, 8, stride=4), :]
-                value = jnp.where(sub < spread(count[pl.ds(col, 1), :]), value, 0.0)
-            else:
-                value = vel[pl.ds((field - 4) * 32 + col, 8, stride=4), :]
-            own[col * 7 + field] = value
+            value = water_tile(pos, vel, mass, count, col, field)
             for layer in range(2):
                 at = rim_lane(field, layer, col)
                 low = jnp.where(lane == at, roll(value, at - layer), low)
                 high = jnp.where(lane == at, roll(value, at - 126 - layer), high)
     for field in range(7):
-        if field < 3:
-            value = gpos[pl.ds(field * 8, 8), :]
-        elif field < 6:
-            value = gvel[pl.ds((field - 3) * 8, 8), :]
-        else:
-            value = grad[...]
-        own[Y_GRAIN + field] = value
+        value = grain_tile(gpos, gvel, grad, field)
         at = GRAIN_LANE + field
         low = jnp.where(lane == at, roll(value, at), low)
         high = jnp.where(lane == at, roll(value, at - 127), high)
@@ -190,7 +205,7 @@
         jnp.where(lane < 64, one, pltpu.roll(roll(one, 64), 4, 0))[0:4] for one in (low, high)
     ]
     for peer in range(16):
-        send[pl.ds(peer * 12 + 8, 4), :] = jnp.where(peer < place[2], low, high)
+        send[pl.ds(peer * 12 + 8, 4), :] = jnp.where(peer < layer_here, low, high)
 
 
 def rim_kernel(place, arrived, own_in, own):
@@ -802,10 +817,19 @@
     ).astype(jnp.int32)
     radius = grain_radius.reshape(8, 128)
     route_grain = iface_grain.reshape(16, 128)
-    send, own = call(
+    bricks = (
+        sph_pos.reshape(96, 128),
+        sph_vel.reshape(96, 128),
+        sph_mass.reshape(32, 128),
+        cell_count.reshape(4, 128),
+        grain_pos.reshape(24, 128),
+        grain_vel.reshape(24, 128),
+        radius,
+    )
+    send = call(
         pack_kernel,
-        [shape(192, 128), shape(Y_TILES, 8, 128)],
-        ins=[S, S] + [pl.BlockSpec(memory_space=pltpu.HBM)] * 9,
+        shape(192, 128),
+        ins=[S] + [pl.BlockSpec(memory_space=pltpu.HBM)] * 9,
         scratch=[pltpu.VMEM((rows, 128), F32) for rows in (96, 96, 32)]
         + [pltpu.VMEM((4, 128), jnp.int32)]
         + [pltpu.VMEM((rows, 128), F32) for rows in (24, 24, 8)]
@@ -813,19 +837,10 @@
         + [pltpu.SemaphoreType.DMA((9,))],
         cost=cost(3),
         limit=None,
-    )(
-        place,
-        pair_count.reshape(16),
-        sph_pos.reshape(96, 128),
-        sph_vel.reshape(96, 128),
-        sph_mass.reshape(32, 128),
-        cell_count.reshape(4, 128),
-        grain_pos.reshape(24, 128),
-        grain_vel.reshape(24, 128),
-        radius,
-        route_grain,
-        iface_offset.reshape(48, 128),
-    )
+    )(pair_count.reshape(16), *bricks, route_grain, iface_offset.reshape(48, 128))
+    later = lax.optimization_barrier((send,) + bricks)
+    send, bricks = later[0], later[1:]
+    own = call(gather_kernel, shape(Y_TILES, 8, 128), ins=[V] * 7, cost=cost(1))(*bricks)
     arrived = lax.all_to_all(
         send.reshape(16, 3, 4, 128), "gz", split_axis=0, concat_axis=0, tiled=True
     ).reshape(48, 4, 128)

time: 75.8 us -> 74.7 us (0.985)
  blocking collectives: 28.3 us -> 0 us
  starting transfers between devices: 14.7 us -> 30.1 us
  waiting for transfers between devices: 4.39 us -> 16.6 us
    all_to_all x1 -> x0, blocking collectives: 28.3 us -> none  [body(): lax.all_to_all(send.reshape(16, 3, 4, 128), 'gz', split_axis=0, concat_ax...]
    all_to_all x0 -> x1, starting transfers between devices: none -> 15.4 us  [body(): lax.all_to_all(send.reshape(16, 3, 4, 128), 'gz', split_axis=0, concat_ax...]
    all_to_all x0 -> x1, waiting for transfers between devices: none -> 12.2 us  [body(): lax.all_to_all(send.reshape(16, 3, 4, 128), 'gz', split_axis=0, concat_ax...]
    pallas_call x1 -> x2, Pallas kernels: 2.56 us -> 2.55 us  [the longest x1 2.54 us: body(): call(pack_kernel, shape(192, 128), ins=[S] + [pl.BlockSpec(memory_space=p...]
  transfers between devices with their start and end apart: 7 -> 8, of which waited for: 1 -> 2; matrix products, arithmetic and copies ran while one was open for 0% -> 0% of each run, Pallas kernels for 23% -> 24%
where the time goes in v2:
time: 74.7 us; the launch traced here: 74.2 us
  starting transfers between devices  30.1 us (40%)
  Pallas kernels  25.2 us (34%)
  waiting for transfers between devices  16.6 us (22%)
  between operations  1.55 us (2%)
    all_to_all x1, starting transfers between devices, body(): lax.all_to_all(send.reshape(16, 3, 4, 128), 'gz', split_axis=0, concat_ax...  15.4 us
    all_to_all x1, waiting for transfers between devices, body(): lax.all_to_all(send.reshape(16, 3, 4, 128), 'gz', split_axis=0, concat_ax...  12.2 us
    pallas_call x1, Pallas kernels, body(): call(force_kernel, shape(96, 128), ins=[S] + [V] * 9, scratch=[pltpu.VMEM...  6.85 us
    ppermute x4, starting transfers between devices, along_x(): lax.ppermute(value, 'gx', [(i, (i + step) % count) for i in range(count)])  5.92 us
    ppermute x2, starting transfers between devices, along_y(): return lax.ppermute(value, 'gy', pairs)  4.68 us
    ppermute x2, waiting for transfers between devices, along_y(): return lax.ppermute(value, 'gy', pairs)  4.38 us
    all_to_all x1, starting transfers between devices, body(): lax.all_to_all(send_back, 'gz', split_axis=0, concat_axis=0, tiled=True)  4.14 us
    pallas_call x1, Pallas kernels, body(): call(mid_density_kernel, [shape(9, 8, 128), shape(4, 8, 128)], ins=[V] *...  3.69 us
  transfers between devices with their start and end apart: 8, of which 2 were waited for; matrix products, arithmetic and copies ran while one was open for 0% of the time, Pallas kernels for 24%

profile of v2, /device:TPU:32, one launch (start us, length us, event | category | flops | bytes accessed | tf_op | source)
XLA Modules:
  0.0 74.2 jit_solution(13963171455298166774)
XLA Ops:
  0.6 2.5 %shard_map.148 = f32[192,128]{1,0:T(8,128)} custom-call(s32[16]{0:T(128)} %bitcast.46, f32[96,128]{1,0:T(8,128)} %bitcast.24, f32[96,128]{1,0:T(8,128)} %bitcast.26, f32[32,128]{1,0:T(8,128)} %bitcast.28, s32[4,128]{1,0:T(4,128)} %bitcast.40, f32[24,128]{1,0:T(8,128)} %bitcast.31, f32[24,128]{1,0:T(8,128)} %bitcast.33, f32[8,128]{1,0:T(8,128)} %bitcast.35, ...), custom_call_target="tpu_custom_call" | custom-call | flops 12000000 | bytes 6000000 | tf_op jit(solution)/shard_map/pallas_call | solution.py:829
  3.2 0.0 copy-start
  3.2 0.0 copy-start.1
  3.2 0.0 copy-start.4
  3.2 0.0 copy-start.5
  3.2 0.0 copy-start.6
  3.2 0.0 copy-start.8
  3.3 15.4 %all-to-all-start = ((f32[16,3,4,128]{3,2,1,0:T(4,128)}), f32[16,3,4,128]{3,2,1,0:T(4,128)S(1)}, u32[]{:S(2)}, u32[]{:S(2)}) async-start(f32[16,3,4,128]{3,2,1,0:T(4,128)} %bitcast.43), calls=%async_computation | async-start | bytes 196608 | tf_op jit(solution)/shard_map/all_to_all | solution.py:844
  18.7 0.6 copy-done.2
  19.3 0.1 pad_add_fusion.place
  19.4 12.2 %all-to-all-done = f32[16,3,4,128]{3,2,1,0:T(4,128)S(1)} async-done(((f32[16,3,4,128]{3,2,1,0:T(4,128)}), f32[16,3,4,128]{3,2,1,0:T(4,128)S(1)}, u32[]{:S(2)}, u32[]{:S(2)}) %all-to-all-start) | async-done | bytes 98336 | tf_op jit(solution)/shard_map/all_to_all | solution.py:844
  31.6 0.7 shard_map.150.own
  32.3 3.4 %collective-permute-start = (f32[37,8,128]{2,1,0:T(8,128)S(1)}, f32[37,8,128]{2,1,0:T(8,128)S(1)}, u32[]{:S(2)}, u32[]{:S(2)}) collective-permute-start(f32[37,8,128]{2,1,0:T(8,128)S(1)} %shard_map.150.own), channel_id=1, source_target_pairs={{0,16},{16,32},{32,48},{1,17},{17,33},{33,49},{2,18},{18,34},{34,5... | collective-permute-start | bytes 454664 | tf_op jit(solution)/shard_map/ppermute | solution.py:792
  35.7 1.3 %collective-permute-start.1 = (f32[37,8,128]{2,1,0:T(8,128)S(1)}, f32[37,8,128]{2,1,0:T(8,128)S(1)}, u32[]{:S(2)}, u32[]{:S(2)}) collective-permute-start(f32[37,8,128]{2,1,0:T(8,128)S(1)} %shard_map.150.own), channel_id=1, source_target_pairs={{16,0},{32,16},{48,32},{17,1},{33,17},{49,33},{18,2},{34,18},{50,3... | collective-permute-start | bytes 454664 | tf_op jit(solution)/shard_map/ppermute | solution.py:792
  37.0 1.4 %shard_map.151.start = f32[9,8,128]{2,1,0:T(8,128)S(1)} custom-call(f32[37,8,128]{2,1,0:T(8,128)S(1)} %shard_map.150.own), custom_call_target="tpu_custom_call" | custom-call | flops 12000000 | bytes 6000000 | tf_op jit(solution)/shard_map/pallas_call | solution.py:858
  38.4 4.4 %collective-permute-done.1.behind = f32[37,8,128]{2,1,0:T(8,128)S(1)} collective-permute-done((f32[37,8,128]{2,1,0:T(8,128)S(1)}, f32[37,8,128]{2,1,0:T(8,128)S(1)}, u32[]{:S(2)}, u32[]{:S(2)}) %collective-permute-start.1) | collective-permute-done | bytes 151584 | tf_op jit(solution)/shard_map/ppermute | solution.py:792
  42.8 0.1 shard_map.152
  42.8 0.0 collective-permute-start.2
  42.9 2.9 %collective-permute-start.3 = (f32[49,8,128]{2,1,0:T(8,128)S(1)}, f32[49,8,128]{2,1,0:T(8,128)S(1)}, u32[]{:S(2)}, u32[]{:S(2)}) collective-permute-start(f32[49,8,128]{2,1,0:T(8,128)S(1)} %get-tuple-element.33), channel_id=1, source_target_pairs={{0,448},{64,0},{128,64},{192,128},{256,192},{320,256},{384,320},{4... | collective-permute-start | bytes 602120 | tf_op jit(solution)/shard_map/ppermute | solution.py:797
  45.8 3.7 %shard_map.153 = (f32[9,8,128]{2,1,0:T(8,128)S(1)}, f32[4,8,128]{2,1,0:T(8,128)S(1)}) custom-call(f32[37,8,128]{2,1,0:T(8,128)S(1)} %shard_map.150.own, f32[37,8,128]{2,1,0:T(8,128)S(1)} %collective-permute-done.ahead, f32[37,8,128]{2,1,0:T(8,128)S(1)} %collective-permute-done.1.behind, f32[9,8,128]{2,1,0:T(8,128)S(1)} %shard_map.151.start), custom_call_target="tpu_custom_call" | custom-call | flops 24000000 | bytes 12000000 | tf_op jit(solution)/shard_map/pallas_call | solution.py:874
  49.5 0.0 collective-permute-done.2.left
  49.5 0.0 copy-start.9
  49.5 1.7 %shard_map.154.own_fields.fields = f32[12,8,128]{2,1,0:T(8,128)S(1)} custom-call(s32[3]{0:T(128)S(1)} %pad_add_fusion.place, f32[37,8,128]{2,1,0:T(8,128)S(1)} %shard_map.150.own, f32[37,8,128]{2,1,0:T(8,128)S(1)} %collective-permute-done.ahead, f32[37,8,128]{2,1,0:T(8,128)S(1)} %collective-permute-done.1.behind, ...), custom_call_target="tpu_custom_call" | custom-call | flops 8000000 | bytes 4000000 | tf_op jit(solution)/shard_map/pallas_call | solution.py:881
  51.3 1.6 %shard_map.156 = (f32[16,4,128]{2,1,0:T(4,128)}, f32[12,8,128]{2,1,0:T(8,128)S(1)}) custom-call(f32[37,8,128]{2,1,0:T(8,128)S(1)} %shard_map.150.own, f32[12,8,128]{2,1,0:T(8,128)S(1)} %shard_map.154.own_fields.fields, f32[48,4,128]{2,1,0:T(4,128)S(1)} %bitcast.23, s32[16,128]{1,0:T(8,128)S(1)} %bitcast.42), custom_call_target="tpu_custom_call" | custom-call | flops 12000000 | bytes 6000000 | tf_op jit(solution)/shard_map/pallas_call | solution.py:888
  52.9 4.1 %all-to-all-start.1 = ((f32[16,4,128]{2,1,0:T(4,128)}), f32[16,4,128]{2,1,0:T(4,128)S(1)}, u32[]{:S(2)}, u32[]{:S(2)}) async-start(f32[16,4,128]{2,1,0:T(4,128)} %get-tuple-element.38), calls=%async_computation.1 | async-start | bytes 65536 | tf_op jit(solution)/shard_map/all_to_all | solution.py:904
  57.1 2.4 %shard_map.155.fields = f32[18,8,128]{2,1,0:T(8,128)S(1)} custom-call(s32[3]{0:T(128)S(1)} %pad_add_fusion.place, f32[37,8,128]{2,1,0:T(8,128)S(1)} %shard_map.150.own, f32[37,8,128]{2,1,0:T(8,128)S(1)} %collective-permute-done.ahead, f32[37,8,128]{2,1,0:T(8,128)S(1)} %collective-permute-done.1.behind, f32[49,8,128]{2,1,0:T(8,128)S(1)} %collective-permute-done.2.left, ...), custom_call_target="tpu_custom_call" | custom-call | flops 12000000 | bytes 6000000 | tf_op jit(solution)/shard_map/pallas_call | solution.py:895
  59.5 0.0 collective-permute-start.4
  59.5 2.9 %collective-permute-start.5 = (f32[18,8,128]{2,1,0:T(8,128)S(1)}, f32[18,8,128]{2,1,0:T(8,128)S(1)}, u32[]{:S(2)}, u32[]{:S(2)}) collective-permute-start(f32[18,8,128]{2,1,0:T(8,128)S(1)} %shard_map.155.fields), channel_id=1, source_target_pairs={{0,448},{64,0},{128,64},{192,128},{256,192},{320,256},{384,320},{4... | collective-permute-start | bytes 221192 | tf_op jit(solution)/shard_map/ppermute | solution.py:797
  63.1 3.2 %shard_map.158.contact = f32[9,8,128]{2,1,0:T(8,128)S(1)} custom-call(s32[3]{0:T(128)S(1)} %pad_add_fusion.place, s32[1]{0:T(128)} %bitcast.21.live_count, f32[37,8,128]{2,1,0:T(8,128)S(1)} %shard_map.150.own, f32[37,8,128]{2,1,0:T(8,128)S(1)} %collective-permute-done.ahead, f32[37,8,128]{2,1,0:T(8,128)S(1)} %collective-permute-done.1.behind, ...), custom_call_target="tpu_custom_call" | custom-call | flops 24000000 | bytes 12000000 | tf_op jit(solution)/shard_map/pallas_call | solution.py:905
  66.4 0.0 copy-start.7
  66.4 6.9 %shard_map.157 = f32[96,128]{1,0:T(8,128)} custom-call(s32[3]{0:T(128)S(1)} %pad_add_fusion.place, f32[37,8,128]{2,1,0:T(8,128)S(1)} %shard_map.150.own, f32[37,8,128]{2,1,0:T(8,128)S(1)} %collective-permute-done.ahead, f32[37,8,128]{2,1,0:T(8,128)S(1)} %collective-permute-done.1.behind, f32[49,8,128]{2,1,0:T(8,128)S(1)} %collective-permute-done.2.left, ...), custom_call_target="tpu_custom_call" | custom-call | flops 24000000 | bytes 12000000 | tf_op jit(solution)/shard_map/pallas_call | solution.py:927
  73.2 1.0 %shard_map.159 = (f32[24,128]{1,0:T(8,128)}, f32[48,128]{1,0:T(8,128)}) custom-call(f32[16,4,128]{2,1,0:T(4,128)S(1)} %all-to-all-done.1.back, s32[16,128]{1,0:T(8,128)S(1)} %bitcast.39, f32[9,8,128]{2,1,0:T(8,128)S(1)} %shard_map.158.contact, f32[8,128]{1,0:T(8,128)S(1)} %bitcast.37), custom_call_target="tpu_custom_call" | custom-call | flops 8000000 | bytes 4000000 | tf_op jit(solution)/shard_map/pallas_call | solution.py:934
  (17 shorter events, 0.0 us)
Async XLA Ops:
  3.2 15.4 %copy-start = (f32[3,8,2,2,128]{4,3,2,1,0:T(2,128)S(1)}, f32[3,8,2,2,128]{4,3,2,1,0:T(2,128)}, u32[]{:S(2)}) copy-start(f32[3,8,2,2,128]{4,3,2,1,0:T(2,128)} %param.13) | copy-start | bytes 147460
  3.2 15.4 %copy-start.1 = (f32[3,8,2,2,128]{4,3,2,1,0:T(2,128)S(1)}, f32[3,8,2,2,128]{4,3,2,1,0:T(2,128)}, u32[]{:S(2)}) copy-start(f32[3,8,2,2,128]{4,3,2,1,0:T(2,128)} %param.14) | copy-start | bytes 147460
  3.2 15.4 %copy-start.4 = (f32[3,2,2,2,128]{4,3,2,1,0:T(2,128)S(1)}, f32[3,2,2,2,128]{4,3,2,1,0:T(2,128)}, u32[]{:S(2)}) copy-start(f32[3,2,2,2,128]{4,3,2,1,0:T(2,128)} %param.17) | copy-start | bytes 36868
  3.2 15.4 %copy-start.5 = (f32[3,2,2,2,128]{4,3,2,1,0:T(2,128)S(1)}, f32[3,2,2,2,128]{4,3,2,1,0:T(2,128)}, u32[]{:S(2)}) copy-start(f32[3,2,2,2,128]{4,3,2,1,0:T(2,128)} %param.18) | copy-start | bytes 36868
  3.2 15.4 %copy-start.6 = (f32[2,2,2,128]{3,2,1,0:T(2,128)S(1)}, f32[2,2,2,128]{3,2,1,0:T(2,128)}, u32[]{:S(2)}) copy-start(f32[2,2,2,128]{3,2,1,0:T(2,128)} %param.19) | copy-start | bytes 12292
  3.2 15.4 %copy-start.8 = (s32[2,2,128]{2,1,0:T(2,128)S(1)}, s32[2,2,128]{2,1,0:T(2,128)}, u32[]{:S(2)}) copy-start(s32[2,2,128]{2,1,0:T(2,128)} %param.16) | copy-start | bytes 6148
  3.3 28.3 %all-to-all-start = ((f32[16,3,4,128]{3,2,1,0:T(4,128)}), f32[16,3,4,128]{3,2,1,0:T(4,128)S(1)}, u32[]{:S(2)}, u32[]{:S(2)}) async-start(f32[16,3,4,128]{3,2,1,0:T(4,128)} %bitcast.43), calls=%async_computation | async-start | bytes 196608 | tf_op jit(solution)/shard_map/all_to_all | solution.py:844
  18.6 0.7 copy-start.2
  32.3 6.1 %collective-permute-start = (f32[37,8,128]{2,1,0:T(8,128)S(1)}, f32[37,8,128]{2,1,0:T(8,128)S(1)}, u32[]{:S(2)}, u32[]{:S(2)}) collective-permute-start(f32[37,8,128]{2,1,0:T(8,128)S(1)} %shard_map.150.own), channel_id=1, source_target_pairs={{0,16},{16,32},{32,48},{1,17},{17,33},{33,49},{2,18},{18,34},{34,5... | collective-permute-start | bytes 454664 | tf_op jit(solution)/shard_map/ppermute | solution.py:792
  35.7 7.1 %collective-permute-start.1 = (f32[37,8,128]{2,1,0:T(8,128)S(1)}, f32[37,8,128]{2,1,0:T(8,128)S(1)}, u32[]{:S(2)}, u32[]{:S(2)}) collective-permute-start(f32[37,8,128]{2,1,0:T(8,128)S(1)} %shard_map.150.own), channel_id=1, source_target_pairs={{16,0},{32,16},{48,32},{17,1},{33,17},{49,33},{18,2},{34,18},{50,3... | collective-permute-start | bytes 454664 | tf_op jit(solution)/shard_map/ppermute | solution.py:792
  42.8 6.7 %collective-permute-start.2 = (f32[49,8,128]{2,1,0:T(8,128)S(1)}, f32[49,8,128]{2,1,0:T(8,128)S(1)}, u32[]{:S(2)}, u32[]{:S(2)}) collective-permute-start(f32[49,8,128]{2,1,0:T(8,128)S(1)} %get-tuple-element.32), channel_id=1, source_target_pairs={{0,64},{64,128},{128,192},{192,256},{256,320},{320,384},{384,448},... | collective-permute-start | bytes 602120 | tf_op jit(solution)/shard_map/ppermute | solution.py:797
  42.9 6.7 %collective-permute-start.3 = (f32[49,8,128]{2,1,0:T(8,128)S(1)}, f32[49,8,128]{2,1,0:T(8,128)S(1)}, u32[]{:S(2)}, u32[]{:S(2)}) collective-permute-start(f32[49,8,128]{2,1,0:T(8,128)S(1)} %get-tuple-element.33), channel_id=1, source_target_pairs={{0,448},{64,0},{128,64},{192,128},{256,192},{320,256},{384,320},{4... | collective-permute-start | bytes 602120 | tf_op jit(solution)/shard_map/ppermute | solution.py:797
  49.5 1.7 %copy-start.9 = (s32[1,1,16,128]{3,2,1,0:T(8,128)S(1)}, s32[1,1,16,128]{3,2,1,0:T(8,128)}, u32[]{:S(2)}) copy-start(s32[1,1,16,128]{3,2,1,0:T(8,128)} %param.25) | copy-start | bytes 24580
  52.9 20.3 %all-to-all-start.1 = ((f32[16,4,128]{2,1,0:T(4,128)}), f32[16,4,128]{2,1,0:T(4,128)S(1)}, u32[]{:S(2)}, u32[]{:S(2)}) async-start(f32[16,4,128]{2,1,0:T(4,128)} %get-tuple-element.38), calls=%async_computation.1 | async-start | bytes 65536 | tf_op jit(solution)/shard_map/all_to_all | solution.py:904
  57.1 6.1 %copy-start.3 = (s32[2,1,1,6144]{3,2,1,0:T(1,128)S(1)}, s32[2,1,1,6144]{3,2,1,0:T(1,128)}, u32[]{:S(2)}) copy-start(s32[2,1,1,6144]{3,2,1,0:T(1,128)} %param.20) | copy-start | bytes 147460
  59.5 6.9 %collective-permute-start.4 = (f32[18,8,128]{2,1,0:T(8,128)S(1)}, f32[18,8,128]{2,1,0:T(8,128)S(1)}, u32[]{:S(2)}, u32[]{:S(2)}) collective-permute-start(f32[18,8,128]{2,1,0:T(8,128)S(1)} %shard_map.155.fields), channel_id=1, source_target_pairs={{0,64},{64,128},{128,192},{192,256},{256,320},{320,384},{384,448},... | collective-permute-start | bytes 221192 | tf_op jit(solution)/shard_map/ppermute | solution.py:797
  59.5 6.8 %collective-permute-start.5 = (f32[18,8,128]{2,1,0:T(8,128)S(1)}, f32[18,8,128]{2,1,0:T(8,128)S(1)}, u32[]{:S(2)}, u32[]{:S(2)}) collective-permute-start(f32[18,8,128]{2,1,0:T(8,128)S(1)} %shard_map.155.fields), channel_id=1, source_target_pairs={{0,448},{64,0},{128,64},{192,128},{256,192},{320,256},{384,320},{4... | collective-permute-start | bytes 221192 | tf_op jit(solution)/shard_map/ppermute | solution.py:797
  66.4 6.9 %copy-start.7 = (s32[1,1,16,128]{3,2,1,0:T(8,128)S(1)}, s32[1,1,16,128]{3,2,1,0:T(8,128)}, u32[]{:S(2)}) copy-start(s32[1,1,16,128]{3,2,1,0:T(8,128)} %param.22) | copy-start | bytes 24580

commit v3 on v2

--- a/solution.py
+++ b/solution.py
@@ -356,7 +356,9 @@
                     total = total + (squared * squared) * ((1.25 - reach) * row[3])
             return total
 
-        total_ref[target] = lax.fori_loop(0, width, one_neighbour, total_ref[target])
+        total_ref[target] = lax.fori_loop(
+            0, width, one_neighbour, total_ref[target], unroll=True
+        )
         return carry
 
     lax.fori_loop(0, targets, one_column, 0)
@@ -585,7 +587,7 @@
             return tuple(total)
 
         zero = jnp.zeros((8, 128), F32)
-        total = lax.fori_loop(0, 9, one_neighbour, (zero,) * 7)
+        total = lax.fori_loop(0, 9, one_neighbour, (zero,) * 7, unroll=3)
         live = jnp.where(near[middle + 3] > 0.0, 1.0, 0.0)
         for d in range(3):
             slow = inverse * (near[middle + 6 + d] * total[3] - total[4 + d])

time: 74.7 us -> 73.5 us (0.984)
  Pallas kernels: 25.2 us -> 23.6 us
  transfers between devices with their start and end apart: 8 -> 8, of which waited for: 2 -> 4; matrix products, arithmetic and copies ran while one was open for 0% -> 0% of each run, Pallas kernels for 24% -> 22%
where the time goes in v3:
time: 73.5 us; the launch traced here: 73 us
  starting transfers between devices  30.1 us (41%)
  Pallas kernels  23.6 us (32%)
  waiting for transfers between devices  17 us (23%)
  between operations  1.52 us (2%)
    all_to_all x1, starting transfers between devices, body(): lax.all_to_all(send.reshape(16, 3, 4, 128), 'gz', split_axis=0, concat_ax...  15.4 us
    all_to_all x1, waiting for transfers between devices, body(): lax.all_to_all(send.reshape(16, 3, 4, 128), 'gz', split_axis=0, concat_ax...  12.2 us
    pallas_call x1, Pallas kernels, body(): call(force_kernel, shape(96, 128), ins=[S] + [V] * 9, scratch=[pltpu.VMEM...  6.34 us
    ppermute x4, starting transfers between devices, along_x(): lax.ppermute(value, 'gx', [(i, (i + step) % count) for i in range(count)])  5.92 us
    ppermute x2, starting transfers between devices, along_y(): return lax.ppermute(value, 'gy', pairs)  4.68 us
    ppermute x2, waiting for transfers between devices, along_y(): return lax.ppermute(value, 'gy', pairs)  4.61 us
    all_to_all x1, starting transfers between devices, body(): lax.all_to_all(send_back, 'gz', split_axis=0, concat_axis=0, tiled=True)  4.14 us
    pallas_call x1, Pallas kernels, body(): call(contact_kernel, shape(9, 8, 128), ins=[S, S] + [V] * 6, scratch=[plt...  3.22 us
  transfers between devices with their start and end apart: 8, of which 4 were waited for; matrix products, arithmetic and copies ran while one was open for 0% of the time, Pallas kernels for 22%

profile of v3, /device:TPU:32, one launch (start us, length us, event | category | flops | bytes accessed | tf_op | source)
XLA Modules:
  0.0 73.0 jit_solution(741218439626516192)
XLA Ops:
  0.6 2.5 %shard_map.148 = f32[192,128]{1,0:T(8,128)} custom-call(s32[16]{0:T(128)} %bitcast.46, f32[96,128]{1,0:T(8,128)} %bitcast.24, f32[96,128]{1,0:T(8,128)} %bitcast.26, f32[32,128]{1,0:T(8,128)} %bitcast.28, s32[4,128]{1,0:T(4,128)} %bitcast.40, f32[24,128]{1,0:T(8,128)} %bitcast.31, f32[24,128]{1,0:T(8,128)} %bitcast.33, f32[8,128]{1,0:T(8,128)} %bitcast.35, ...), custom_call_target="tpu_custom_call" | custom-call | flops 12000000 | bytes 6000000 | tf_op jit(solution)/shard_map/pallas_call | solution.py:831
  3.2 0.0 copy-start
  3.2 0.0 copy-start.1
  3.2 0.0 copy-start.4
  3.2 0.0 copy-start.5
  3.2 0.0 copy-start.6
  3.2 0.0 copy-start.8
  3.3 15.4 %all-to-all-start = ((f32[16,3,4,128]{3,2,1,0:T(4,128)}), f32[16,3,4,128]{3,2,1,0:T(4,128)S(1)}, u32[]{:S(2)}, u32[]{:S(2)}) async-start(f32[16,3,4,128]{3,2,1,0:T(4,128)} %bitcast.43), calls=%async_computation | async-start | bytes 196608 | tf_op jit(solution)/shard_map/all_to_all | solution.py:846
  18.7 0.6 copy-done.2
  19.3 0.1 pad_add_fusion.place
  19.4 12.2 %all-to-all-done = f32[16,3,4,128]{3,2,1,0:T(4,128)S(1)} async-done(((f32[16,3,4,128]{3,2,1,0:T(4,128)}), f32[16,3,4,128]{3,2,1,0:T(4,128)S(1)}, u32[]{:S(2)}, u32[]{:S(2)}) %all-to-all-start) | async-done | bytes 98336 | tf_op jit(solution)/shard_map/all_to_all | solution.py:846
  31.6 0.7 shard_map.150.own
  32.3 3.4 %collective-permute-start = (f32[37,8,128]{2,1,0:T(8,128)S(1)}, f32[37,8,128]{2,1,0:T(8,128)S(1)}, u32[]{:S(2)}, u32[]{:S(2)}) collective-permute-start(f32[37,8,128]{2,1,0:T(8,128)S(1)} %shard_map.150.own), channel_id=1, source_target_pairs={{0,16},{16,32},{32,48},{1,17},{17,33},{33,49},{2,18},{18,34},{34,5... | collective-permute-start | bytes 454664 | tf_op jit(solution)/shard_map/ppermute | solution.py:794
  35.7 1.3 %collective-permute-start.1 = (f32[37,8,128]{2,1,0:T(8,128)S(1)}, f32[37,8,128]{2,1,0:T(8,128)S(1)}, u32[]{:S(2)}, u32[]{:S(2)}) collective-permute-start(f32[37,8,128]{2,1,0:T(8,128)S(1)} %shard_map.150.own), channel_id=1, source_target_pairs={{16,0},{32,16},{48,32},{17,1},{33,17},{49,33},{18,2},{34,18},{50,3... | collective-permute-start | bytes 454664 | tf_op jit(solution)/shard_map/ppermute | solution.py:794
  37.0 1.2 %shard_map.151.start = f32[9,8,128]{2,1,0:T(8,128)S(1)} custom-call(f32[37,8,128]{2,1,0:T(8,128)S(1)} %shard_map.150.own), custom_call_target="tpu_custom_call" | custom-call | flops 12000000 | bytes 6000000 | tf_op jit(solution)/shard_map/pallas_call | solution.py:860
  38.2 0.2 collective-permute-done.ahead
  38.4 4.4 %collective-permute-done.1.behind = f32[37,8,128]{2,1,0:T(8,128)S(1)} collective-permute-done((f32[37,8,128]{2,1,0:T(8,128)S(1)}, f32[37,8,128]{2,1,0:T(8,128)S(1)}, u32[]{:S(2)}, u32[]{:S(2)}) %collective-permute-start.1) | collective-permute-done | bytes 151584 | tf_op jit(solution)/shard_map/ppermute | solution.py:794
  42.8 0.1 shard_map.152
  42.8 0.0 collective-permute-start.2
  42.9 2.9 %collective-permute-start.3 = (f32[49,8,128]{2,1,0:T(8,128)S(1)}, f32[49,8,128]{2,1,0:T(8,128)S(1)}, u32[]{:S(2)}, u32[]{:S(2)}) collective-permute-start(f32[49,8,128]{2,1,0:T(8,128)S(1)} %get-tuple-element.33), channel_id=1, source_target_pairs={{0,448},{64,0},{128,64},{192,128},{256,192},{320,256},{384,320},{4... | collective-permute-start | bytes 602120 | tf_op jit(solution)/shard_map/ppermute | solution.py:799
  45.8 3.2 %shard_map.153 = (f32[9,8,128]{2,1,0:T(8,128)S(1)}, f32[4,8,128]{2,1,0:T(8,128)S(1)}) custom-call(f32[37,8,128]{2,1,0:T(8,128)S(1)} %shard_map.150.own, f32[37,8,128]{2,1,0:T(8,128)S(1)} %collective-permute-done.ahead, f32[37,8,128]{2,1,0:T(8,128)S(1)} %collective-permute-done.1.behind, f32[9,8,128]{2,1,0:T(8,128)S(1)} %shard_map.151.start), custom_call_target="tpu_custom_call" | custom-call | flops 24000000 | bytes 12000000 | tf_op jit(solution)/shard_map/pallas_call | solution.py:876
  49.0 0.2 collective-permute-done.2.left
  49.2 1.5 %shard_map.154.own_fields.fields = f32[12,8,128]{2,1,0:T(8,128)S(1)} custom-call(s32[3]{0:T(128)S(1)} %pad_add_fusion.place, f32[37,8,128]{2,1,0:T(8,128)S(1)} %shard_map.150.own, f32[37,8,128]{2,1,0:T(8,128)S(1)} %collective-permute-done.ahead, f32[37,8,128]{2,1,0:T(8,128)S(1)} %collective-permute-done.1.behind, ...), custom_call_target="tpu_custom_call" | custom-call | flops 8000000 | bytes 4000000 | tf_op jit(solution)/shard_map/pallas_call | solution.py:883
  50.8 1.6 %shard_map.156 = (f32[16,4,128]{2,1,0:T(4,128)}, f32[12,8,128]{2,1,0:T(8,128)S(1)}) custom-call(f32[37,8,128]{2,1,0:T(8,128)S(1)} %shard_map.150.own, f32[12,8,128]{2,1,0:T(8,128)S(1)} %shard_map.154.own_fields.fields, f32[48,4,128]{2,1,0:T(4,128)S(1)} %bitcast.23, s32[16,128]{1,0:T(8,128)S(1)} %bitcast.42), custom_call_target="tpu_custom_call" | custom-call | flops 12000000 | bytes 6000000 | tf_op jit(solution)/shard_map/pallas_call | solution.py:890
  52.4 4.1 %all-to-all-start.1 = ((f32[16,4,128]{2,1,0:T(4,128)}), f32[16,4,128]{2,1,0:T(4,128)S(1)}, u32[]{:S(2)}, u32[]{:S(2)}) async-start(f32[16,4,128]{2,1,0:T(4,128)} %get-tuple-element.38), calls=%async_computation.1 | async-start | bytes 65536 | tf_op jit(solution)/shard_map/all_to_all | solution.py:906
  56.6 2.2 %shard_map.155.fields = f32[18,8,128]{2,1,0:T(8,128)S(1)} custom-call(s32[3]{0:T(128)S(1)} %pad_add_fusion.place, f32[37,8,128]{2,1,0:T(8,128)S(1)} %shard_map.150.own, f32[37,8,128]{2,1,0:T(8,128)S(1)} %collective-permute-done.ahead, f32[37,8,128]{2,1,0:T(8,128)S(1)} %collective-permute-done.1.behind, f32[49,8,128]{2,1,0:T(8,128)S(1)} %collective-permute-done.2.left, ...), custom_call_target="tpu_custom_call" | custom-call | flops 12000000 | bytes 6000000 | tf_op jit(solution)/shard_map/pallas_call | solution.py:897
  58.8 0.0 collective-permute-start.4
  58.8 2.9 %collective-permute-start.5 = (f32[18,8,128]{2,1,0:T(8,128)S(1)}, f32[18,8,128]{2,1,0:T(8,128)S(1)}, u32[]{:S(2)}, u32[]{:S(2)}) collective-permute-start(f32[18,8,128]{2,1,0:T(8,128)S(1)} %shard_map.155.fields), channel_id=1, source_target_pairs={{0,448},{64,0},{128,64},{192,128},{256,192},{320,256},{384,320},{4... | collective-permute-start | bytes 221192 | tf_op jit(solution)/shard_map/ppermute | solution.py:799
  62.4 3.2 %shard_map.158.contact = f32[9,8,128]{2,1,0:T(8,128)S(1)} custom-call(s32[3]{0:T(128)S(1)} %pad_add_fusion.place, s32[1]{0:T(128)} %bitcast.21.live_count, f32[37,8,128]{2,1,0:T(8,128)S(1)} %shard_map.150.own, f32[37,8,128]{2,1,0:T(8,128)S(1)} %collective-permute-done.ahead, f32[37,8,128]{2,1,0:T(8,128)S(1)} %collective-permute-done.1.behind, ...), custom_call_target="tpu_custom_call" | custom-call | flops 24000000 | bytes 12000000 | tf_op jit(solution)/shard_map/pallas_call | solution.py:907
  65.7 0.0 copy-start.7
  65.7 6.3 %shard_map.157 = f32[96,128]{1,0:T(8,128)} custom-call(s32[3]{0:T(128)S(1)} %pad_add_fusion.place, f32[37,8,128]{2,1,0:T(8,128)S(1)} %shard_map.150.own, f32[37,8,128]{2,1,0:T(8,128)S(1)} %collective-permute-done.ahead, f32[37,8,128]{2,1,0:T(8,128)S(1)} %collective-permute-done.1.behind, f32[49,8,128]{2,1,0:T(8,128)S(1)} %collective-permute-done.2.left, ...), custom_call_target="tpu_custom_call" | custom-call | flops 24000000 | bytes 12000000 | tf_op jit(solution)/shard_map/pallas_call | solution.py:929
  72.0 1.0 %shard_map.159 = (f32[24,128]{1,0:T(8,128)}, f32[48,128]{1,0:T(8,128)}) custom-call(f32[16,4,128]{2,1,0:T(4,128)S(1)} %all-to-all-done.1.back, s32[16,128]{1,0:T(8,128)S(1)} %bitcast.39, f32[9,8,128]{2,1,0:T(8,128)S(1)} %shard_map.158.contact, f32[8,128]{1,0:T(8,128)S(1)} %bitcast.37), custom_call_target="tpu_custom_call" | custom-call | flops 8000000 | bytes 4000000 | tf_op jit(solution)/shard_map/pallas_call | solution.py:936
  (17 shorter events, 0.0 us)
Async XLA Ops:
  3.2 15.4 %copy-start = (f32[3,8,2,2,128]{4,3,2,1,0:T(2,128)S(1)}, f32[3,8,2,2,128]{4,3,2,1,0:T(2,128)}, u32[]{:S(2)}) copy-start(f32[3,8,2,2,128]{4,3,2,1,0:T(2,128)} %param.13) | copy-start | bytes 147460
  3.2 15.4 %copy-start.1 = (f32[3,8,2,2,128]{4,3,2,1,0:T(2,128)S(1)}, f32[3,8,2,2,128]{4,3,2,1,0:T(2,128)}, u32[]{:S(2)}) copy-start(f32[3,8,2,2,128]{4,3,2,1,0:T(2,128)} %param.14) | copy-start | bytes 147460
  3.2 15.4 %copy-start.4 = (f32[3,2,2,2,128]{4,3,2,1,0:T(2,128)S(1)}, f32[3,2,2,2,128]{4,3,2,1,0:T(2,128)}, u32[]{:S(2)}) copy-start(f32[3,2,2,2,128]{4,3,2,1,0:T(2,128)} %param.17) | copy-start | bytes 36868
  3.2 15.4 %copy-start.5 = (f32[3,2,2,2,128]{4,3,2,1,0:T(2,128)S(1)}, f32[3,2,2,2,128]{4,3,2,1,0:T(2,128)}, u32[]{:S(2)}) copy-start(f32[3,2,2,2,128]{4,3,2,1,0:T(2,128)} %param.18) | copy-start | bytes 36868
  3.2 15.4 %copy-start.6 = (f32[2,2,2,128]{3,2,1,0:T(2,128)S(1)}, f32[2,2,2,128]{3,2,1,0:T(2,128)}, u32[]{:S(2)}) copy-start(f32[2,2,2,128]{3,2,1,0:T(2,128)} %param.19) | copy-start | bytes 12292
  3.2 15.4 %copy-start.8 = (s32[2,2,128]{2,1,0:T(2,128)S(1)}, s32[2,2,128]{2,1,0:T(2,128)}, u32[]{:S(2)}) copy-start(s32[2,2,128]{2,1,0:T(2,128)} %param.16) | copy-start | bytes 6148
  3.3 28.3 %all-to-all-start = ((f32[16,3,4,128]{3,2,1,0:T(4,128)}), f32[16,3,4,128]{3,2,1,0:T(4,128)S(1)}, u32[]{:S(2)}, u32[]{:S(2)}) async-start(f32[16,3,4,128]{3,2,1,0:T(4,128)} %bitcast.43), calls=%async_computation | async-start | bytes 196608 | tf_op jit(solution)/shard_map/all_to_all | solution.py:846
  18.6 0.7 copy-start.2
  32.3 6.1 %collective-permute-start = (f32[37,8,128]{2,1,0:T(8,128)S(1)}, f32[37,8,128]{2,1,0:T(8,128)S(1)}, u32[]{:S(2)}, u32[]{:S(2)}) collective-permute-start(f32[37,8,128]{2,1,0:T(8,128)S(1)} %shard_map.150.own), channel_id=1, source_target_pairs={{0,16},{16,32},{32,48},{1,17},{17,33},{33,49},{2,18},{18,34},{34,5... | collective-permute-start | bytes 454664 | tf_op jit(solution)/shard_map/ppermute | solution.py:794
  35.7 7.1 %collective-permute-start.1 = (f32[37,8,128]{2,1,0:T(8,128)S(1)}, f32[37,8,128]{2,1,0:T(8,128)S(1)}, u32[]{:S(2)}, u32[]{:S(2)}) collective-permute-start(f32[37,8,128]{2,1,0:T(8,128)S(1)} %shard_map.150.own), channel_id=1, source_target_pairs={{16,0},{32,16},{48,32},{17,1},{33,17},{49,33},{18,2},{34,18},{50,3... | collective-permute-start | bytes 454664 | tf_op jit(solution)/shard_map/ppermute | solution.py:794
  42.8 6.4 %collective-permute-start.2 = (f32[49,8,128]{2,1,0:T(8,128)S(1)}, f32[49,8,128]{2,1,0:T(8,128)S(1)}, u32[]{:S(2)}, u32[]{:S(2)}) collective-permute-start(f32[49,8,128]{2,1,0:T(8,128)S(1)} %get-tuple-element.32), channel_id=1, source_target_pairs={{0,64},{64,128},{128,192},{192,256},{256,320},{320,384},{384,448},... | collective-permute-start | bytes 602120 | tf_op jit(solution)/shard_map/ppermute | solution.py:799
  42.9 6.3 %collective-permute-start.3 = (f32[49,8,128]{2,1,0:T(8,128)S(1)}, f32[49,8,128]{2,1,0:T(8,128)S(1)}, u32[]{:S(2)}, u32[]{:S(2)}) collective-permute-start(f32[49,8,128]{2,1,0:T(8,128)S(1)} %get-tuple-element.33), channel_id=1, source_target_pairs={{0,448},{64,0},{128,64},{192,128},{256,192},{320,256},{384,320},{4... | collective-permute-start | bytes 602120 | tf_op jit(solution)/shard_map/ppermute | solution.py:799
  49.2 1.6 %copy-start.9 = (s32[1,1,16,128]{3,2,1,0:T(8,128)S(1)}, s32[1,1,16,128]{3,2,1,0:T(8,128)}, u32[]{:S(2)}) copy-start(s32[1,1,16,128]{3,2,1,0:T(8,128)} %param.25) | copy-start | bytes 24580
  52.4 19.6 %all-to-all-start.1 = ((f32[16,4,128]{2,1,0:T(4,128)}), f32[16,4,128]{2,1,0:T(4,128)S(1)}, u32[]{:S(2)}, u32[]{:S(2)}) async-start(f32[16,4,128]{2,1,0:T(4,128)} %get-tuple-element.38), calls=%async_computation.1 | async-start | bytes 65536 | tf_op jit(solution)/shard_map/all_to_all | solution.py:906
  56.6 5.9 %copy-start.3 = (s32[2,1,1,6144]{3,2,1,0:T(1,128)S(1)}, s32[2,1,1,6144]{3,2,1,0:T(1,128)}, u32[]{:S(2)}) copy-start(s32[2,1,1,6144]{3,2,1,0:T(1,128)} %param.20) | copy-start | bytes 147460
  58.8 6.9 %collective-permute-start.4 = (f32[18,8,128]{2,1,0:T(8,128)S(1)}, f32[18,8,128]{2,1,0:T(8,128)S(1)}, u32[]{:S(2)}, u32[]{:S(2)}) collective-permute-start(f32[18,8,128]{2,1,0:T(8,128)S(1)} %shard_map.155.fields), channel_id=1, source_target_pairs={{0,64},{64,128},{128,192},{192,256},{256,320},{320,384},{384,448},... | collective-permute-start | bytes 221192 | tf_op jit(solution)/shard_map/ppermute | solution.py:799
  58.8 6.8 %collective-permute-start.5 = (f32[18,8,128]{2,1,0:T(8,128)S(1)}, f32[18,8,128]{2,1,0:T(8,128)S(1)}, u32[]{:S(2)}, u32[]{:S(2)}) collective-permute-start(f32[18,8,128]{2,1,0:T(8,128)S(1)} %shard_map.155.fields), channel_id=1, source_target_pairs={{0,448},{64,0},{128,64},{192,128},{256,192},{320,256},{384,320},{4... | collective-permute-start | bytes 221192 | tf_op jit(solution)/shard_map/ppermute | solution.py:799
  65.7 6.4 %copy-start.7 = (s32[1,1,16,128]{3,2,1,0:T(8,128)S(1)}, s32[1,1,16,128]{3,2,1,0:T(8,128)}, u32[]{:S(2)}) copy-start(s32[1,1,16,128]{3,2,1,0:T(8,128)} %param.22) | copy-start | bytes 24580

commit v4 on v3

--- a/solution.py
+++ b/solution.py
@@ -587,7 +587,7 @@
             return tuple(total)
 
         zero = jnp.zeros((8, 128), F32)
-        total = lax.fori_loop(0, 9, one_neighbour, (zero,) * 7, unroll=3)
+        total = lax.fori_loop(0, 9, one_neighbour, (zero,) * 7, unroll=True)
         live = jnp.where(near[middle + 3] > 0.0, 1.0, 0.0)
         for d in range(3):
             slow = inverse * (near[middle + 6 + d] * total[3] - total[4 + d])

time: 73.5 us -> 73.8 us (level)
  no operation moved by 1% of the time
where the time goes in v4:
time: 73.8 us; the launch traced here: 73.4 us
  starting transfers between devices  30.1 us (41%)
  Pallas kernels  24 us (33%)
  waiting for transfers between devices  17 us (23%)
  between operations  1.52 us (2%)
    all_to_all x1, starting transfers between devices, body(): lax.all_to_all(send.reshape(16, 3, 4, 128), 'gz', split_axis=0, concat_ax...  15.4 us
    all_to_all x1, waiting for transfers between devices, body(): lax.all_to_all(send.reshape(16, 3, 4, 128), 'gz', split_axis=0, concat_ax...  12.2 us
    pallas_call x1, Pallas kernels, body(): call(force_kernel, shape(96, 128), ins=[S] + [V] * 9, scratch=[pltpu.VMEM...  6.7 us
    ppermute x4, starting transfers between devices, along_x(): lax.ppermute(value, 'gx', [(i, (i + step) % count) for i in range(count)])  5.92 us
    ppermute x2, starting transfers between devices, along_y(): return lax.ppermute(value, 'gy', pairs)  4.68 us
    ppermute x2, waiting for transfers between devices, along_y(): return lax.ppermute(value, 'gy', pairs)  4.61 us
    all_to_all x1, starting transfers between devices, body(): lax.all_to_all(send_back, 'gz', split_axis=0, concat_axis=0, tiled=True)  4.14 us
    pallas_call x1, Pallas kernels, body(): call(contact_kernel, shape(9, 8, 128), ins=[S, S] + [V] * 6, scratch=[plt...  3.22 us
  transfers between devices with their start and end apart: 8, of which 4 were waited for; matrix products, arithmetic and copies ran while one was open for 0% of the time, Pallas kernels for 22%

profile of v4, /device:TPU:32, one launch (start us, length us, event | category | flops | bytes accessed | tf_op | source)
XLA Modules:
  0.0 73.4 jit_solution(11202546142934577882)
XLA Ops:
  0.6 2.5 %shard_map.148 = f32[192,128]{1,0:T(8,128)} custom-call(s32[16]{0:T(128)} %bitcast.46, f32[96,128]{1,0:T(8,128)} %bitcast.24, f32[96,128]{1,0:T(8,128)} %bitcast.26, f32[32,128]{1,0:T(8,128)} %bitcast.28, s32[4,128]{1,0:T(4,128)} %bitcast.40, f32[24,128]{1,0:T(8,128)} %bitcast.31, f32[24,128]{1,0:T(8,128)} %bitcast.33, f32[8,128]{1,0:T(8,128)} %bitcast.35, ...), custom_call_target="tpu_custom_call" | custom-call | flops 12000000 | bytes 6000000 | tf_op jit(solution)/shard_map/pallas_call | solution.py:831
  3.2 0.0 copy-start
  3.2 0.0 copy-start.1
  3.2 0.0 copy-start.4
  3.2 0.0 copy-start.5
  3.2 0.0 copy-start.6
  3.2 0.0 copy-start.8
  3.3 15.4 %all-to-all-start = ((f32[16,3,4,128]{3,2,1,0:T(4,128)}), f32[16,3,4,128]{3,2,1,0:T(4,128)S(1)}, u32[]{:S(2)}, u32[]{:S(2)}) async-start(f32[16,3,4,128]{3,2,1,0:T(4,128)} %bitcast.43), calls=%async_computation | async-start | bytes 196608 | tf_op jit(solution)/shard_map/all_to_all | solution.py:846
  18.7 0.6 copy-done.2
  19.3 0.1 pad_add_fusion.place
  19.4 12.2 %all-to-all-done = f32[16,3,4,128]{3,2,1,0:T(4,128)S(1)} async-done(((f32[16,3,4,128]{3,2,1,0:T(4,128)}), f32[16,3,4,128]{3,2,1,0:T(4,128)S(1)}, u32[]{:S(2)}, u32[]{:S(2)}) %all-to-all-start) | async-done | bytes 98336 | tf_op jit(solution)/shard_map/all_to_all | solution.py:846
  31.6 0.7 shard_map.150.own
  32.3 3.4 %collective-permute-start = (f32[37,8,128]{2,1,0:T(8,128)S(1)}, f32[37,8,128]{2,1,0:T(8,128)S(1)}, u32[]{:S(2)}, u32[]{:S(2)}) collective-permute-start(f32[37,8,128]{2,1,0:T(8,128)S(1)} %shard_map.150.own), channel_id=1, source_target_pairs={{0,16},{16,32},{32,48},{1,17},{17,33},{33,49},{2,18},{18,34},{34,5... | collective-permute-start | bytes 454664 | tf_op jit(solution)/shard_map/ppermute | solution.py:794
  35.7 1.3 %collective-permute-start.1 = (f32[37,8,128]{2,1,0:T(8,128)S(1)}, f32[37,8,128]{2,1,0:T(8,128)S(1)}, u32[]{:S(2)}, u32[]{:S(2)}) collective-permute-start(f32[37,8,128]{2,1,0:T(8,128)S(1)} %shard_map.150.own), channel_id=1, source_target_pairs={{16,0},{32,16},{48,32},{17,1},{33,17},{49,33},{18,2},{34,18},{50,3... | collective-permute-start | bytes 454664 | tf_op jit(solution)/shard_map/ppermute | solution.py:794
  37.0 1.2 %shard_map.151.start = f32[9,8,128]{2,1,0:T(8,128)S(1)} custom-call(f32[37,8,128]{2,1,0:T(8,128)S(1)} %shard_map.150.own), custom_call_target="tpu_custom_call" | custom-call | flops 12000000 | bytes 6000000 | tf_op jit(solution)/shard_map/pallas_call | solution.py:860
  38.2 0.2 collective-permute-done.ahead
  38.4 4.4 %collective-permute-done.1.behind = f32[37,8,128]{2,1,0:T(8,128)S(1)} collective-permute-done((f32[37,8,128]{2,1,0:T(8,128)S(1)}, f32[37,8,128]{2,1,0:T(8,128)S(1)}, u32[]{:S(2)}, u32[]{:S(2)}) %collective-permute-start.1) | collective-permute-done | bytes 151584 | tf_op jit(solution)/shard_map/ppermute | solution.py:794
  42.8 0.1 shard_map.152
  42.8 0.0 collective-permute-start.2
  42.9 2.9 %collective-permute-start.3 = (f32[49,8,128]{2,1,0:T(8,128)S(1)}, f32[49,8,128]{2,1,0:T(8,128)S(1)}, u32[]{:S(2)}, u32[]{:S(2)}) collective-permute-start(f32[49,8,128]{2,1,0:T(8,128)S(1)} %get-tuple-element.33), channel_id=1, source_target_pairs={{0,448},{64,0},{128,64},{192,128},{256,192},{320,256},{384,320},{4... | collective-permute-start | bytes 602120 | tf_op jit(solution)/shard_map/ppermute | solution.py:799
  45.8 3.2 %shard_map.153 = (f32[9,8,128]{2,1,0:T(8,128)S(1)}, f32[4,8,128]{2,1,0:T(8,128)S(1)}) custom-call(f32[37,8,128]{2,1,0:T(8,128)S(1)} %shard_map.150.own, f32[37,8,128]{2,1,0:T(8,128)S(1)} %collective-permute-done.ahead, f32[37,8,128]{2,1,0:T(8,128)S(1)} %collective-permute-done.1.behind, f32[9,8,128]{2,1,0:T(8,128)S(1)} %shard_map.151.start), custom_call_target="tpu_custom_call" | custom-call | flops 24000000 | bytes 12000000 | tf_op jit(solution)/shard_map/pallas_call | solution.py:876
  49.0 0.2 collective-permute-done.2.left
  49.2 1.5 %shard_map.154.own_fields.fields = f32[12,8,128]{2,1,0:T(8,128)S(1)} custom-call(s32[3]{0:T(128)S(1)} %pad_add_fusion.place, f32[37,8,128]{2,1,0:T(8,128)S(1)} %shard_map.150.own, f32[37,8,128]{2,1,0:T(8,128)S(1)} %collective-permute-done.ahead, f32[37,8,128]{2,1,0:T(8,128)S(1)} %collective-permute-done.1.behind, ...), custom_call_target="tpu_custom_call" | custom-call | flops 8000000 | bytes 4000000 | tf_op jit(solution)/shard_map/pallas_call | solution.py:883
  50.8 1.6 %shard_map.156 = (f32[16,4,128]{2,1,0:T(4,128)}, f32[12,8,128]{2,1,0:T(8,128)S(1)}) custom-call(f32[37,8,128]{2,1,0:T(8,128)S(1)} %shard_map.150.own, f32[12,8,128]{2,1,0:T(8,128)S(1)} %shard_map.154.own_fields.fields, f32[48,4,128]{2,1,0:T(4,128)S(1)} %bitcast.23, s32[16,128]{1,0:T(8,128)S(1)} %bitcast.42), custom_call_target="tpu_custom_call" | custom-call | flops 12000000 | bytes 6000000 | tf_op jit(solution)/shard_map/pallas_call | solution.py:890
  52.4 4.1 %all-to-all-start.1 = ((f32[16,4,128]{2,1,0:T(4,128)}), f32[16,4,128]{2,1,0:T(4,128)S(1)}, u32[]{:S(2)}, u32[]{:S(2)}) async-start(f32[16,4,128]{2,1,0:T(4,128)} %get-tuple-element.38), calls=%async_computation.1 | async-start | bytes 65536 | tf_op jit(solution)/shard_map/all_to_all | solution.py:906
  56.6 2.2 %shard_map.155.fields = f32[18,8,128]{2,1,0:T(8,128)S(1)} custom-call(s32[3]{0:T(128)S(1)} %pad_add_fusion.place, f32[37,8,128]{2,1,0:T(8,128)S(1)} %shard_map.150.own, f32[37,8,128]{2,1,0:T(8,128)S(1)} %collective-permute-done.ahead, f32[37,8,128]{2,1,0:T(8,128)S(1)} %collective-permute-done.1.behind, f32[49,8,128]{2,1,0:T(8,128)S(1)} %collective-permute-done.2.left, ...), custom_call_target="tpu_custom_call" | custom-call | flops 12000000 | bytes 6000000 | tf_op jit(solution)/shard_map/pallas_call | solution.py:897
  58.8 0.0 collective-permute-start.4
  58.8 2.9 %collective-permute-start.5 = (f32[18,8,128]{2,1,0:T(8,128)S(1)}, f32[18,8,128]{2,1,0:T(8,128)S(1)}, u32[]{:S(2)}, u32[]{:S(2)}) collective-permute-start(f32[18,8,128]{2,1,0:T(8,128)S(1)} %shard_map.155.fields), channel_id=1, source_target_pairs={{0,448},{64,0},{128,64},{192,128},{256,192},{320,256},{384,320},{4... | collective-permute-start | bytes 221192 | tf_op jit(solution)/shard_map/ppermute | solution.py:799
  62.4 3.2 %shard_map.158.contact = f32[9,8,128]{2,1,0:T(8,128)S(1)} custom-call(s32[3]{0:T(128)S(1)} %pad_add_fusion.place, s32[1]{0:T(128)} %bitcast.21.live_count, f32[37,8,128]{2,1,0:T(8,128)S(1)} %shard_map.150.own, f32[37,8,128]{2,1,0:T(8,128)S(1)} %collective-permute-done.ahead, f32[37,8,128]{2,1,0:T(8,128)S(1)} %collective-permute-done.1.behind, ...), custom_call_target="tpu_custom_call" | custom-call | flops 24000000 | bytes 12000000 | tf_op jit(solution)/shard_map/pallas_call | solution.py:907
  65.7 0.0 copy-start.7
  65.7 6.7 %shard_map.157 = f32[96,128]{1,0:T(8,128)} custom-call(s32[3]{0:T(128)S(1)} %pad_add_fusion.place, f32[37,8,128]{2,1,0:T(8,128)S(1)} %shard_map.150.own, f32[37,8,128]{2,1,0:T(8,128)S(1)} %collective-permute-done.ahead, f32[37,8,128]{2,1,0:T(8,128)S(1)} %collective-permute-done.1.behind, f32[49,8,128]{2,1,0:T(8,128)S(1)} %collective-permute-done.2.left, ...), custom_call_target="tpu_custom_call" | custom-call | flops 24000000 | bytes 12000000 | tf_op jit(solution)/shard_map/pallas_call | solution.py:929
  72.4 1.0 %shard_map.159 = (f32[24,128]{1,0:T(8,128)}, f32[48,128]{1,0:T(8,128)}) custom-call(f32[16,4,128]{2,1,0:T(4,128)S(1)} %all-to-all-done.1.back, s32[16,128]{1,0:T(8,128)S(1)} %bitcast.39, f32[9,8,128]{2,1,0:T(8,128)S(1)} %shard_map.158.contact, f32[8,128]{1,0:T(8,128)S(1)} %bitcast.37), custom_call_target="tpu_custom_call" | custom-call | flops 8000000 | bytes 4000000 | tf_op jit(solution)/shard_map/pallas_call | solution.py:936
  (17 shorter events, 0.0 us)
Async XLA Ops:
  3.2 15.4 %copy-start = (f32[3,8,2,2,128]{4,3,2,1,0:T(2,128)S(1)}, f32[3,8,2,2,128]{4,3,2,1,0:T(2,128)}, u32[]{:S(2)}) copy-start(f32[3,8,2,2,128]{4,3,2,1,0:T(2,128)} %param.13) | copy-start | bytes 147460
  3.2 15.4 %copy-start.1 = (f32[3,8,2,2,128]{4,3,2,1,0:T(2,128)S(1)}, f32[3,8,2,2,128]{4,3,2,1,0:T(2,128)}, u32[]{:S(2)}) copy-start(f32[3,8,2,2,128]{4,3,2,1,0:T(2,128)} %param.14) | copy-start | bytes 147460
  3.2 15.4 %copy-start.4 = (f32[3,2,2,2,128]{4,3,2,1,0:T(2,128)S(1)}, f32[3,2,2,2,128]{4,3,2,1,0:T(2,128)}, u32[]{:S(2)}) copy-start(f32[3,2,2,2,128]{4,3,2,1,0:T(2,128)} %param.17) | copy-start | bytes 36868
  3.2 15.4 %copy-start.5 = (f32[3,2,2,2,128]{4,3,2,1,0:T(2,128)S(1)}, f32[3,2,2,2,128]{4,3,2,1,0:T(2,128)}, u32[]{:S(2)}) copy-start(f32[3,2,2,2,128]{4,3,2,1,0:T(2,128)} %param.18) | copy-start | bytes 36868
  3.2 15.4 %copy-start.6 = (f32[2,2,2,128]{3,2,1,0:T(2,128)S(1)}, f32[2,2,2,128]{3,2,1,0:T(2,128)}, u32[]{:S(2)}) copy-start(f32[2,2,2,128]{3,2,1,0:T(2,128)} %param.19) | copy-start | bytes 12292
  3.2 15.4 %copy-start.8 = (s32[2,2,128]{2,1,0:T(2,128)S(1)}, s32[2,2,128]{2,1,0:T(2,128)}, u32[]{:S(2)}) copy-start(s32[2,2,128]{2,1,0:T(2,128)} %param.16) | copy-start | bytes 6148
  3.3 28.3 %all-to-all-start = ((f32[16,3,4,128]{3,2,1,0:T(4,128)}), f32[16,3,4,128]{3,2,1,0:T(4,128)S(1)}, u32[]{:S(2)}, u32[]{:S(2)}) async-start(f32[16,3,4,128]{3,2,1,0:T(4,128)} %bitcast.43), calls=%async_computation | async-start | bytes 196608 | tf_op jit(solution)/shard_map/all_to_all | solution.py:846
  18.6 0.7 copy-start.2
  32.3 6.1 %collective-permute-start = (f32[37,8,128]{2,1,0:T(8,128)S(1)}, f32[37,8,128]{2,1,0:T(8,128)S(1)}, u32[]{:S(2)}, u32[]{:S(2)}) collective-permute-start(f32[37,8,128]{2,1,0:T(8,128)S(1)} %shard_map.150.own), channel_id=1, source_target_pairs={{0,16},{16,32},{32,48},{1,17},{17,33},{33,49},{2,18},{18,34},{34,5... | collective-permute-start | bytes 454664 | tf_op jit(solution)/shard_map/ppermute | solution.py:794
  35.7 7.1 %collective-permute-start.1 = (f32[37,8,128]{2,1,0:T(8,128)S(1)}, f32[37,8,128]{2,1,0:T(8,128)S(1)}, u32[]{:S(2)}, u32[]{:S(2)}) collective-permute-start(f32[37,8,128]{2,1,0:T(8,128)S(1)} %shard_map.150.own), channel_id=1, source_target_pairs={{16,0},{32,16},{48,32},{17,1},{33,17},{49,33},{18,2},{34,18},{50,3... | collective-permute-start | bytes 454664 | tf_op jit(solution)/shard_map/ppermute | solution.py:794
  42.8 6.4 %collective-permute-start.2 = (f32[49,8,128]{2,1,0:T(8,128)S(1)}, f32[49,8,128]{2,1,0:T(8,128)S(1)}, u32[]{:S(2)}, u32[]{:S(2)}) collective-permute-start(f32[49,8,128]{2,1,0:T(8,128)S(1)} %get-tuple-element.32), channel_id=1, source_target_pairs={{0,64},{64,128},{128,192},{192,256},{256,320},{320,384},{384,448},... | collective-permute-start | bytes 602120 | tf_op jit(solution)/shard_map/ppermute | solution.py:799
  42.9 6.3 %collective-permute-start.3 = (f32[49,8,128]{2,1,0:T(8,128)S(1)}, f32[49,8,128]{2,1,0:T(8,128)S(1)}, u32[]{:S(2)}, u32[]{:S(2)}) collective-permute-start(f32[49,8,128]{2,1,0:T(8,128)S(1)} %get-tuple-element.33), channel_id=1, source_target_pairs={{0,448},{64,0},{128,64},{192,128},{256,192},{320,256},{384,320},{4... | collective-permute-start | bytes 602120 | tf_op jit(solution)/shard_map/ppermute | solution.py:799
  49.2 1.6 %copy-start.9 = (s32[1,1,16,128]{3,2,1,0:T(8,128)S(1)}, s32[1,1,16,128]{3,2,1,0:T(8,128)}, u32[]{:S(2)}) copy-start(s32[1,1,16,128]{3,2,1,0:T(8,128)} %param.25) | copy-start | bytes 24580
  52.4 20.0 %all-to-all-start.1 = ((f32[16,4,128]{2,1,0:T(4,128)}), f32[16,4,128]{2,1,0:T(4,128)S(1)}, u32[]{:S(2)}, u32[]{:S(2)}) async-start(f32[16,4,128]{2,1,0:T(4,128)} %get-tuple-element.38), calls=%async_computation.1 | async-start | bytes 65536 | tf_op jit(solution)/shard_map/all_to_all | solution.py:906
  56.6 5.9 %copy-start.3 = (s32[2,1,1,6144]{3,2,1,0:T(1,128)S(1)}, s32[2,1,1,6144]{3,2,1,0:T(1,128)}, u32[]{:S(2)}) copy-start(s32[2,1,1,6144]{3,2,1,0:T(1,128)} %param.20) | copy-start | bytes 147460
  58.8 6.9 %collective-permute-start.4 = (f32[18,8,128]{2,1,0:T(8,128)S(1)}, f32[18,8,128]{2,1,0:T(8,128)S(1)}, u32[]{:S(2)}, u32[]{:S(2)}) collective-permute-start(f32[18,8,128]{2,1,0:T(8,128)S(1)} %shard_map.155.fields), channel_id=1, source_target_pairs={{0,64},{64,128},{128,192},{192,256},{256,320},{320,384},{384,448},... | collective-permute-start | bytes 221192 | tf_op jit(solution)/shard_map/ppermute | solution.py:799
  58.8 6.8 %collective-permute-start.5 = (f32[18,8,128]{2,1,0:T(8,128)S(1)}, f32[18,8,128]{2,1,0:T(8,128)S(1)}, u32[]{:S(2)}, u32[]{:S(2)}) collective-permute-start(f32[18,8,128]{2,1,0:T(8,128)S(1)} %shard_map.155.fields), channel_id=1, source_target_pairs={{0,448},{64,0},{128,64},{192,128},{256,192},{320,256},{384,320},{4... | collective-permute-start | bytes 221192 | tf_op jit(solution)/shard_map/ppermute | solution.py:799
  65.7 6.7 %copy-start.7 = (s32[1,1,16,128]{3,2,1,0:T(8,128)S(1)}, s32[1,1,16,128]{3,2,1,0:T(8,128)}, u32[]{:S(2)}) copy-start(s32[1,1,16,128]{3,2,1,0:T(8,128)} %param.22) | copy-start | bytes 24580
